TPU v7x, 512 devices: a whole 4x4x16 slice. The times are simulated.
512 devices in a mesh: dp: 32 (over y, x, core), tensor: 16 (over z).
Axes of the slice: x: 4, y: 4, z: 16, core: 2. Of those that a mesh axis runs over, the one named last changes fastest.
Arguments:
- attn_out: bfloat16 [3, 2048, 4096], P(None, 'dp', 'tensor'), may hold values from -6 to 6
- base_weight: bfloat16 [4096, 4096], P('tensor'), may hold values from -0.09375 to 0.09375
- store_a: bfloat16 [128, 4096, 128], P('dp', 'tensor'), may hold values from -0.09375 to 0.09375
- store_b: bfloat16 [128, 128, 4096], P('dp', None, 'tensor'), may hold values from -0.5 to 0.5
- adapter_lists: int32 [32, 16], P('dp'), may hold values from 0 to 127, as said below
- placement_map: int32 [128], replicated, may hold values from 0 to 127, as said below
- request_slot: int32 [2048], P('dp'), may hold values from 0 to 15
Outputs:
- projected: bfloat16 [3, 2048, 4096], P(None, 'dp', 'tensor')
Inputs may be any that keep to these rules, and one draw needn't show every extreme that they name: `adapter_lists`: each replica's 16 adapters are stored on 16 different indices of dp. `placement_map` is a permutation; adapter a's panels are row placement_map[a] of the stores, held by index placement_map[a] // 4 of dp.
All inputs are finite; a program needn't handle non-finite values.
Results may differ from a plain program's by a relative error of at most 0.001.
Values may be sent and summed in bfloat16 or wider, within the bound.
No kernel may reach another device: no remote copies, remote signals or barrier semaphores. Data moves between devices by JAX's collectives and lax.ppermute only.
A program may use at most 64 MiB of HBM per device.

v0:
```python
import jax
import jax.numpy as jnp
from jax import lax
from jax.sharding import PartitionSpec as P


def on_device(attn_out, base_weight, store_a, store_b, adapter_lists, placement_map, request_slot):
    replicas = lax.axis_size("dp")
    stored = store_a.shape[0]
    slot_count = adapter_lists.shape[1]
    rank_width = store_a.shape[2]
    requests = request_slot.shape[0]
    catalog = placement_map.shape[0]
    my_list = adapter_lists[0]
    matches = my_list[:, None] == jnp.arange(catalog, dtype=jnp.int32)[None, :]
    position = jnp.sum(jnp.where(matches, placement_map[None, :], 0), axis=1)
    holder = position // stored
    local_slot = position % stored
    devices = jnp.arange(replicas, dtype=jnp.int32)
    wanted = (
        jnp.sum(jnp.where(holder[None, :] == devices[:, None], local_slot[None, :] + 1, 0), axis=1)
        - 1
    )
    every_wish = lax.all_gather(wanted[None, :], "dp", axis=0, tiled=True)
    own_index = lax.axis_index("dp")
    asked_slot = lax.dynamic_index_in_dim(every_wish, own_index, 1, keepdims=False)
    picker = (asked_slot[:, None] == jnp.arange(stored, dtype=jnp.int32)[None, :]).astype(
        jnp.bfloat16
    )
    slot_hit = (request_slot[:, None] == jnp.arange(slot_count, dtype=jnp.int32)[None, :]).astype(
        jnp.float32
    )
    step_results = []
    for step_index in range(attn_out.shape[0]):
        send_a = jnp.einsum(
            "qn,nir->qir", picker, store_a, preferred_element_type=jnp.float32
        ).astype(jnp.bfloat16)
        send_b = jnp.einsum(
            "qn,nro->qro", picker, store_b, preferred_element_type=jnp.float32
        ).astype(jnp.bfloat16)
        recv_a = lax.all_to_all(send_a, "dp", split_axis=0, concat_axis=0, tiled=True)
        recv_b = lax.all_to_all(send_b, "dp", split_axis=0, concat_axis=0, tiled=True)
        slot_a = jnp.take(recv_a, holder, axis=0)
        slot_b = jnp.take(recv_b, holder, axis=0)
        fetch_stack_a = jnp.transpose(slot_a, (1, 0, 2)).reshape(
            slot_a.shape[1], slot_count * rank_width
        )
        fetch_stack_b = slot_b.reshape(slot_count * rank_width, slot_b.shape[2]).astype(jnp.float32)
        step_in = attn_out[step_index]
        base_output_sum = lax.psum_scatter(
            lax.dot_general(
                base_weight, step_in, (((0,), (1,)), ((), ())), preferred_element_type=jnp.float32
            ),
            "tensor",
            scatter_dimension=0,
            tiled=True,
        )
        every_slot = jnp.dot(step_in, fetch_stack_a, preferred_element_type=jnp.float32).reshape(
            requests, slot_count, rank_width
        )
        rank_part = jnp.sum(every_slot * slot_hit[:, :, None], axis=1)
        rank_reduce = lax.psum(rank_part, "tensor")
        spread = (slot_hit[:, :, None] * rank_reduce[:, None, :]).reshape(
            requests, slot_count * rank_width
        )
        low_rank_delta = jnp.dot(
            spread,
            fetch_stack_b,
            precision=lax.Precision.HIGHEST,
            preferred_element_type=jnp.float32,
        )
        step_results.append((base_output_sum.T + low_rank_delta).astype(jnp.bfloat16))
    return jnp.stack(step_results)


def solution(mesh):
    placed = (
        P(None, "dp", "tensor"),
        P("tensor", None),
        P("dp", "tensor", None),
        P("dp", None, "tensor"),
        P("dp", None),
        P(),
        P("dp"),
    )
    return jax.shard_map(
        on_device, mesh=mesh, in_specs=placed, out_specs=P(None, "dp", "tensor"), check_vma=False
    )
```

profile of v0, /device:TPU:6, one launch (start us, length us, event | category | flops | bytes accessed | tf_op | source)
XLA Modules:
  0.0 509.2 jit_solution(18405111244604827407)
XLA Ops:
  6.5 0.0 copy-start
  6.5 1.0 select_reduce_fusion.1
  7.6 0.1 select_reduce_fusion
  7.7 1.3 dynamic-slice
  9.6 0.1 add_dynamic-update-slice_fusion
  9.7 0.1 reshape.118
  9.8 114.3 %all-reduce.1 = s32[32,32]{1,0:T(8,128)S(1)} all-reduce(s32[32,32]{1,0:T(8,128)S(1)} %reshape.118), channel_id=2, replica_groups=mesh['dp'=32,'tensor'=16] {'dp'}, use_global_device_ids=true, to_apply=%add | all-reduce | flops 1024 | bytes 8192
  124.1 0.2 dynamic-slice_reduce_fusion
  124.3 1.7 convolution_convert_fusion.1
  126.0 2.1 copy.40
  128.1 19.8 %all-to-all-start = ((bf16[32,256,128]{2,1,0:T(8,128)(2,1)}), bf16[32,256,128]{2,1,0:T(8,128)(2,1)}, u32[]{:S(2)}, u32[]{:S(2)}) async-start(bf16[32,256,128]{2,1,0:T(8,128)(2,1)} %copy.40), calls=%async_computation.1 | async-start | bytes 4194304 | tf_op jit(solution)/shard_map/all_to_all | solution.py:41
  147.9 0.0 copy-start.3
  148.0 0.0 reduce-scatter.4.cloned.1.call-start
  148.0 0.0 copy-done
  148.0 0.0 copy-done.1
  148.0 1.5 fusion.30
  149.5 0.0 reduce-scatter.4.cloned.1.call-update
  149.5 0.0 all-reduce.5.cloned.1.call-start
  149.6 0.0 copy-done.3
  149.6 24.0 %all-to-all-done = bf16[32,256,128]{2,1,0:T(8,128)(2,1)} async-done(((bf16[32,256,128]{2,1,0:T(8,128)(2,1)}), bf16[32,256,128]{2,1,0:T(8,128)(2,1)}, u32[]{:S(2)}, u32[]{:S(2)}) %all-to-all-start) | async-done | bytes 2097184 | tf_op jit(solution)/shard_map/all_to_all | solution.py:41
  173.6 2.3 gather_fusion
  176.0 1.2 select_bitcast_fusion
  177.1 1.5 copy.41
  178.6 0.4 convolution_bitcast_fusion
  179.0 0.4 convolution_bitcast_fusion.1
  179.5 0.4 convolution_bitcast_fusion.2
  179.9 0.8 fusion.11
  180.8 0.0 all-reduce.5.cloned.1.call-update
  180.8 0.0 copy-start.2
  180.8 0.0 reduce-scatter.6.cloned.1.call-start
  180.9 1.5 fusion.27
  182.4 0.0 reduce-scatter.6.cloned.1.call-update
  182.4 0.8 convolution_convert_fusion
  183.2 2.5 copy.44
  185.7 9.0 %all-to-all-start.1 = ((bf16[32,128,256]{2,1,0:T(8,128)(2,1)}), bf16[32,128,256]{2,1,0:T(8,128)(2,1)}, u32[]{:S(2)}, u32[]{:S(2)}) async-start(bf16[32,128,256]{2,1,0:T(8,128)(2,1)} %copy.44), calls=%async_computation.2 | async-start | bytes 4194304 | tf_op jit(solution)/shard_map/all_to_all | solution.py:42
  194.7 0.0 reduce-scatter.8.cloned.1.call-start
  194.8 1.5 fusion.24
  196.2 0.0 reduce-scatter.8.cloned.1.call-update
  196.3 24.1 %all-to-all-done.1 = bf16[32,128,256]{2,1,0:T(8,128)(2,1)} async-done(((bf16[32,128,256]{2,1,0:T(8,128)(2,1)}), bf16[32,128,256]{2,1,0:T(8,128)(2,1)}, u32[]{:S(2)}, u32[]{:S(2)}) %all-to-all-start.1) | async-done | bytes 2097184 | tf_op jit(solution)/shard_map/all_to_all | solution.py:42
  220.4 2.2 gather_fusion.1
  222.6 2.9 reduce-scatter.4.cloned.1.call-done
  225.5 134.9 %all-reduce.5.cloned.1.call-done = (f32[64,128]{1,0:T(8,128)}, f32[64,128]{1,0:T(8,128)}, f32[64,128]{1,0:T(8,128)}) async-done(((f32[64,128]{1,0:T(8,128)}, f32[64,128]{1,0:T(8,128)}, f32[64,128]{1,0:T(8,128)}), (f32[64,128]{1,0:T(8,128)}, f32[64,128]{1,0:T(8,128)}, f32[64,128]{1,0:T(8,128)})) %all-reduce.5.cloned.1.call-update) | async-done | bytes 98320 | tf_op jit(solution)/shard_map/psum | solution.py:62
  360.3 1.6 fusion.6
  362.0 67.5 %reduce-scatter.6.cloned.1.call-done = f32[256,64]{0,1:T(8,128)} async-done(((f32[4096,64]{0,1:T(8,128)}), f32[256,64]{0,1:T(8,128)}) %reduce-scatter.6.cloned.1.call-update) | async-done | bytes 65552 | tf_op jit(solution)/shard_map/reduce_scatter | solution.py:50
  429.4 1.6 fusion.7
  431.0 69.4 %reduce-scatter.8.cloned.1.call-done = f32[256,64]{0,1:T(8,128)} async-done(((f32[4096,64]{0,1:T(8,128)}), f32[256,64]{0,1:T(8,128)}) %reduce-scatter.8.cloned.1.call-update) | async-done | bytes 65552 | tf_op jit(solution)/shard_map/reduce_scatter | solution.py:50
  500.5 1.6 fusion.8
  502.0 0.7 pad_maximum_fusion
  (10 shorter events, 0.1 us)
Async XLA Ops:
  6.5 141.5 %copy-start = (bf16[256,4096]{1,0:T(8,128)(2,1)S(1)}, bf16[256,4096]{1,0:T(8,128)(2,1)}, u32[]{:S(2)}) copy-start(bf16[256,4096]{1,0:T(8,128)(2,1)} %param.12) | copy-start | bytes 6291460
  128.1 19.9 %copy-start.1 = (bf16[3,64,256]{2,1,0:T(8,128)(2,1)S(1)}, bf16[3,64,256]{2,1,0:T(8,128)(2,1)}, u32[]{:S(2)}) copy-start(bf16[3,64,256]{2,1,0:T(8,128)(2,1)} %param.11) | copy-start | bytes 294916
  128.1 45.5 %all-to-all-start = ((bf16[32,256,128]{2,1,0:T(8,128)(2,1)}), bf16[32,256,128]{2,1,0:T(8,128)(2,1)}, u32[]{:S(2)}, u32[]{:S(2)}) async-start(bf16[32,256,128]{2,1,0:T(8,128)(2,1)} %copy.40), calls=%async_computation.1 | async-start | bytes 4194304 | tf_op jit(solution)/shard_map/all_to_all | solution.py:41
  147.9 1.6 copy-start.3
  148.0 77.5 %reduce-scatter.4.cloned.1.call-start = ((), (), s32[]{:S(2)}) async-start(), calls=%async_computation.5 | async-start | bytes 1114112 | tf_op jit(solution)/shard_map/reduce_scatter | solution.py:50
  149.5 210.8 %all-reduce.5.cloned.1.call-start = ((), (), s32[]{:S(2)}) async-start(), calls=%async_computation.8 | async-start | bytes 196608 | tf_op jit(solution)/shard_map/psum | solution.py:62
  180.8 1.6 copy-start.2
  180.8 248.6 %reduce-scatter.6.cloned.1.call-start = ((), (), s32[]{:S(2)}) async-start(), calls=%async_computation.6 | async-start | bytes 1114112 | tf_op jit(solution)/shard_map/reduce_scatter | solution.py:50
  185.7 34.7 %all-to-all-start.1 = ((bf16[32,128,256]{2,1,0:T(8,128)(2,1)}), bf16[32,128,256]{2,1,0:T(8,128)(2,1)}, u32[]{:S(2)}, u32[]{:S(2)}) async-start(bf16[32,128,256]{2,1,0:T(8,128)(2,1)} %copy.44), calls=%async_computation.2 | async-start | bytes 4194304 | tf_op jit(solution)/shard_map/all_to_all | solution.py:42
  194.7 305.7 %reduce-scatter.8.cloned.1.call-start = ((), (), s32[]{:S(2)}) async-start(), calls=%async_computation.7 | async-start | bytes 1114112 | tf_op jit(solution)/shard_map/reduce_scatter | solution.py:50
  360.3 140.1 %copy-start.4 = (f32[64,128]{1,0:T(8,128)S(1)}, f32[64,128]{1,0:T(8,128)}, u32[]{:S(2)}) copy-start(f32[64,128]{1,0:T(8,128)} %get-tuple-element.10) | copy-start | bytes 98308
Sparse Core Ops, SparseCore 0:
  151.6 73.8 reduce-scatter.3
  228.2 132.1 all-reduce.4
  363.1 66.2 reduce-scatter.5
  432.3 68.0 reduce-scatter.7
where the time goes:
time: 510 us; the launch traced here: 509 us
  waiting for transfers between devices  323 us (63%)
  blocking collectives  114 us (22%)
  starting transfers between devices  29 us (6%)
  between operations  13.9 us (3%)
  matrix products  13.1 us (3%)
  local copies, waits for them, and re-layouts  12.2 us (2%)
    reduce_scatter x3, waiting for transfers between devices, on_device(): lax.psum_scatter(lax.dot_general(base_weight, step_in, (((0,), (1,)), (()...  140 us
    psum x1, waiting for transfers between devices, on_device(): rank_reduce = lax.psum(rank_part, 'tensor')  135 us
    unnamed x1, blocking collectives  114 us
    all_to_all x1, waiting for transfers between devices, on_device(): lax.all_to_all(send_b, 'dp', split_axis=0, concat_axis=0, tiled=True)  24.1 us
    all_to_all x1, waiting for transfers between devices, on_device(): lax.all_to_all(send_a, 'dp', split_axis=0, concat_axis=0, tiled=True)  24 us
    all_to_all x1, starting transfers between devices, on_device(): lax.all_to_all(send_a, 'dp', split_axis=0, concat_axis=0, tiled=True)  19.8 us
  transfers between devices with their start and end apart: 6, of which 6 were waited for; matrix products, arithmetic and copies ran while one was open for 4% of the time, Pallas kernels for 0%

commit v1 on v0

v1 whole, which is shorter than its diff:
```python
import jax
import jax.numpy as jnp
from jax import lax
from jax.experimental import pallas as pl
from jax.experimental.pallas import tpu as pltpu
from jax.sharding import PartitionSpec as P

VMEM_BYTES = 24 * 1024 * 1024
WINDOW = 4


def local_call(body, outs, flops, moved, scalars, *arrays, scratch=()):
    smem = pl.BlockSpec(memory_space=pltpu.SMEM)
    vmem = pl.BlockSpec(memory_space=pltpu.VMEM)
    return pl.pallas_call(
        body,
        out_shape=outs,
        in_specs=[smem] * len(scalars) + [vmem] * len(arrays),
        out_specs=jax.tree.map(lambda _: vmem, outs),
        scratch_shapes=list(scratch),
        compiler_params=pltpu.CompilerParams(vmem_limit_bytes=VMEM_BYTES),
        cost_estimate=pl.CostEstimate(flops=flops, bytes_accessed=moved, transcendentals=0),
    )(*scalars, *arrays)


def wish_kernel(stored, list_ref, place_ref, wish_ref):
    wish_ref[...] = jnp.zeros_like(wish_ref)
    for s in range(list_ref.shape[1]):
        position = place_ref[list_ref[0, s]]
        slot = lax.rem(position, stored)
        wish_ref[lax.div(position, stored)] = jnp.full(wish_ref.shape[1:], slot, jnp.int32)


def hold_kernel(stored, steps, list_ref, place_ref, slot_ref, hold_ref):
    requests = slot_ref.shape[0]

    @pl.loop(0, requests, unroll=8)
    def _(r):
        holder = lax.div(place_ref[list_ref[0, slot_ref[r]]], stored)
        for step in range(steps):
            hold_ref[pl.ds(step * requests + r, 1), :] = jnp.full((1, 128), holder, jnp.int32)


def pick_kernel(asked_ref, store_ref, out_ref):
    @pl.loop(0, out_ref.shape[0])
    def _(q):
        out_ref[q] = store_ref[jnp.max(asked_ref[q])]


def turned(me_ref, ref):
    share = ref.shape[0] // WINDOW
    return [
        ref[pl.ds(pl.multiple_of(lax.rem(me_ref[0] + j, WINDOW) * share, share), share), :]
        for j in range(WINDOW)
    ]


def shrink_kernel(me_ref, hold_ref, x_ref, panels_ref, *refs):
    outs, total_ref = refs[:-1], refs[-1]
    hold = jnp.concatenate(turned(me_ref, hold_ref), axis=0)
    x = jnp.concatenate(turned(me_ref, x_ref), axis=0)
    total_ref[...] = jnp.zeros_like(total_ref)

    @pl.loop(0, panels_ref.shape[0], unroll=4)
    def _(q):
        product = jnp.dot(x, panels_ref[q], preferred_element_type=jnp.float32)
        total_ref[...] = jnp.where(hold == q, product, total_ref[...])

    share = total_ref.shape[0] // WINDOW
    for j, out_ref in enumerate(outs):
        out_ref[...] = total_ref[j * share:(j + 1) * share, :]


def final_kernel(me_ref, hold_ref, *refs):
    blocks, (panels_ref, base_ref, out_ref, total_ref) = refs[:WINDOW], refs[WINDOW:]
    hold = jnp.concatenate(turned(me_ref, hold_ref), axis=0)
    hold = jnp.concatenate([hold] * (total_ref.shape[1] // hold.shape[1]), axis=1)
    shrink = jnp.concatenate([b[...] for b in blocks], axis=0)
    high = shrink.astype(jnp.bfloat16)
    low = (shrink - high.astype(jnp.float32)).astype(jnp.bfloat16)
    both = jnp.concatenate([high, low], axis=1)
    total_ref[...] = jnp.zeros_like(total_ref)

    @pl.loop(0, panels_ref.shape[0], unroll=4)
    def _(q):
        panel = panels_ref[q]
        product = jnp.dot(
            both, jnp.concatenate([panel, panel], axis=0), preferred_element_type=jnp.float32
        )
        total_ref[...] = jnp.where(hold == q, product, total_ref[...])

    share = total_ref.shape[0] // WINDOW
    for j in range(WINDOW):
        begin = pl.multiple_of(lax.rem(me_ref[0] + j, WINDOW) * share, share)
        delta = total_ref[j * share:(j + 1) * share, :]
        here = base_ref[pl.ds(begin, share), :] + delta
        out_ref[pl.ds(begin, share), :] = here.astype(out_ref.dtype)


def shift(value, by, size):
    return lax.ppermute(value, "tensor", [(i, (i + by) % size) for i in range(size)])


def sum_over_tensor(parts):
    size = lax.axis_size("tensor")
    near = [shift(parts[1], 1, size), shift(parts[3], -1, size), shift(parts[2], -2, size)]
    mine = (parts[0] + near[0]) + (near[1] + near[2])
    far = [shift(mine, by, size) for by in (8, 4, -4)]
    mine = (mine + far[0]) + (far[1] + far[2])
    return [mine, shift(mine, -1, size), shift(mine, 2, size), shift(mine, 1, size)]


def on_device(attn_out, base_weight, store_a, store_b, adapter_lists, placement_map, request_slot):
    replicas = lax.axis_size("dp")
    columns = lax.axis_size("tensor")
    stored, depth, rank = store_a.shape
    steps, requests, _ = attn_out.shape
    width = store_b.shape[2]
    rows = steps * requests
    share = rows // WINDOW
    f32 = jnp.float32
    me = lax.axis_index("tensor").astype(jnp.int32).reshape(1)
    x = attn_out.reshape(rows, depth)

    wish = local_call(
        lambda *refs: wish_kernel(stored, *refs),
        jax.ShapeDtypeStruct((replicas, 8, 128), jnp.int32), 0, 1 << 17,
        (adapter_lists, placement_map),
    )
    asked = lax.all_to_all(wish, "dp", split_axis=0, concat_axis=0, tiled=True)

    x_later, wish = lax.optimization_barrier((x, wish))
    partial = jnp.einsum("icw,ri->crw", base_weight.reshape(depth, columns, width), x_later,
                         preferred_element_type=f32)
    base = lax.psum_scatter(partial, "tensor", scatter_dimension=0, tiled=True)[0]

    hold = local_call(
        lambda *refs: hold_kernel(stored, steps, *refs),
        jax.ShapeDtypeStruct((rows, 128), jnp.int32), 0, 1 << 17,
        (adapter_lists, placement_map, request_slot),
    )

    def fetch(store):
        shape = (replicas,) + store.shape[1:]
        picked = local_call(
            pick_kernel, jax.ShapeDtypeStruct(shape, store.dtype), 0, 5 << 20, (), asked, store
        )
        return lax.all_to_all(picked, "dp", split_axis=0, concat_axis=0, tiled=True)

    got_a = fetch(store_a)
    got_b = fetch(store_b)
    parts = local_call(
        shrink_kernel, (jax.ShapeDtypeStruct((share, rank), f32),) * WINDOW,
        2 * rows * replicas * depth * rank, 3 << 20, (me,), hold, x, got_a,
        scratch=(pltpu.VMEM((rows, rank), f32),),
    )
    shrink = sum_over_tensor(parts)
    out = local_call(
        final_kernel, jax.ShapeDtypeStruct((rows, width), jnp.bfloat16),
        4 * rows * replicas * rank * width, 3 << 20, (me,), hold, *shrink, got_b, base,
        scratch=(pltpu.VMEM((rows, width), f32),),
    )
    return out.reshape(steps, requests, width)


def solution(mesh):
    placed = (
        P(None, "dp", "tensor"),
        P("tensor", None),
        P("dp", "tensor", None),
        P("dp", None, "tensor"),
        P("dp", None),
        P(),
        P("dp"),
    )
    return jax.shard_map(
        on_device, mesh=mesh, in_specs=placed, out_specs=P(None, "dp", "tensor"), check_vma=False
    )
```

time: 510 us -> 147 us (0.29)
  waiting for transfers between devices: 323 us -> 27.5 us
  blocking collectives: 114 us -> 14.8 us
  starting transfers between devices: 29 us -> 60.2 us
  Pallas kernels: 0 us -> 22.3 us
  matrix products: 13.1 us -> 3.87 us
  local copies, waits for them, and re-layouts: 12.2 us -> 3.64 us
    reduce_scatter x3 -> x1, waiting for transfers between devices: 140 us -> 0.01 us  [on_device(): lax.psum_scatter(partial, 'tensor', scatter_dimension=0, tiled=True)[0]]
    psum x1 -> x0, waiting for transfers between devices: 135 us -> none  [on_device(): rank_reduce = lax.psum(rank_part, 'tensor')]
    unnamed x1 -> x0, blocking collectives: 114 us -> none
    ppermute x0 -> x9, starting transfers between devices: none -> 45.4 us  [shift(): lax.ppermute(value, 'tensor', [(i, (i + by) % size) for i in range(size)])]
    all_to_all x2, waiting for transfers between devices: 48.1 us -> 17.8 us  [fetch(): return lax.all_to_all(picked, 'dp', split_axis=0, concat_axis=0, tiled=True)]
    pallas_call x0 -> x6, Pallas kernels: none -> 22.3 us  [local_call(): pl.pallas_call(body, out_shape=outs, in_specs=[smem] * len(scalars) + [vm...]
    all_to_all x0 -> x1, blocking collectives: none -> 14.8 us  [on_device(): asked = lax.all_to_all(wish, 'dp', split_axis=0, concat_axis=0, tiled=True)]
    all_to_all x2, starting transfers between devices: 28.9 us -> 14.8 us  [fetch(): return lax.all_to_all(picked, 'dp', split_axis=0, concat_axis=0, tiled=True)]
  transfers between devices with their start and end apart: 6 -> 12, of which waited for: 6 -> 5; matrix products, arithmetic and copies ran while one was open for 4% -> 0% of each run, Pallas kernels for 0% -> 12%
where the time goes in v1:
time: 147 us; the launch traced here: 146 us
  starting transfers between devices  60.2 us (41%)
  waiting for transfers between devices  27.5 us (19%)
  Pallas kernels  22.3 us (15%)
  blocking collectives  14.8 us (10%)
  between operations  13.6 us (9%)
  matrix products  3.87 us (3%)
  local copies, waits for them, and re-layouts  3.64 us (2%)
    ppermute x9, starting transfers between devices, shift(): lax.ppermute(value, 'tensor', [(i, (i + by) % size) for i in range(size)])  45.4 us
    pallas_call x6, Pallas kernels, local_call(): pl.pallas_call(body, out_shape=outs, in_specs=[smem] * len(scalars) + [vm...  22.3 us
    all_to_all x2, waiting for transfers between devices, fetch(): return lax.all_to_all(picked, 'dp', split_axis=0, concat_axis=0, tiled=True)  17.8 us
    all_to_all x2, starting transfers between devices, fetch(): return lax.all_to_all(picked, 'dp', split_axis=0, concat_axis=0, tiled=True)  14.8 us
    all_to_all x1, blocking collectives, on_device(): asked = lax.all_to_all(wish, 'dp', split_axis=0, concat_axis=0, tiled=True)  14.8 us
    ppermute x9, waiting for transfers between devices, shift(): lax.ppermute(value, 'tensor', [(i, (i + by) % size) for i in range(size)])  9.67 us
    dot_general x1, matrix products, on_device(): jnp.einsum('icw,ri->crw', base_weight.reshape(depth, columns, width), x_l...  3.87 us
    unnamed x20, local copies, waits for them, and re-layouts  3.64 us
  transfers between devices with their start and end apart: 12, of which 5 were waited for; matrix products, arithmetic and copies ran while one was open for 0% of the time, Pallas kernels for 12%

profile of v1, /device:TPU:6, one launch (start us, length us, event | category | flops | bytes accessed | tf_op | source)
XLA Modules:
  0.0 145.9 jit_solution(10305516154685641223)
XLA Ops:
  6.5 0.0 reduce-scatter.2.cloned.1.call-start
  6.5 0.0 copy-start.4
  6.5 0.7 copy-done.4
  7.2 0.0 copy-start.6
  7.2 0.7 copy-done.6
  7.8 0.6 shard_map.74
  8.5 3.9 %fusion.3 = f32[16,192,256]{2,1,0:T(8,128)} fusion(bf16[32,16,8,256]{3,2,1,0:T(8,128)(2,1)} %bitcast.18, bf16[192,256]{1,0:T(8,128)(2,1)} %bitcast.15), kind=kOutput, calls=%fused_computation.3 | convolution fusion | flops 402653184 | bytes 5341184 | tf_op jit(solution)/shard_map/icw,ri->crw/dot_general | solution.py:133
  12.3 0.0 copy-start.2
  12.3 0.0 reduce-scatter.2.cloned.1.call-update
  12.4 14.8 %all_to_all.15.asked_ref = s32[32,8,128]{2,1,0:T(8,128)S(1)} all-to-all(s32[32,8,128]{2,1,0:T(8,128)S(1)} %shard_map.74), channel_id=1, replica_groups=mesh['dp'=32,'tensor'=16] {'dp'}, dimensions={0} | all-to-all | bytes 262144 | tf_op jit(solution)/shard_map/all_to_all | solution.py:130
  27.2 0.0 copy-done.2
  27.2 6.5 %shard_map.75 = bf16[32,256,128]{2,1,0:T(8,128)(2,1)S(1)} custom-call(s32[32,8,128]{2,1,0:T(8,128)S(1)} %all_to_all.15.asked_ref, bf16[4,256,128]{2,1,0:T(8,128)(2,1)S(1)} %copy-done.2), custom_call_target="tpu_custom_call" | custom-call | bytes 5242880 | tf_op jit(solution)/shard_map/pallas_call | solution.py:15
  33.6 0.0 copy-start
  33.6 1.4 copy-done
  35.0 0.0 copy-start.3
  35.0 5.8 %all-to-all-start.1 = ((bf16[32,256,128]{2,1,0:T(8,128)(2,1)}), bf16[32,256,128]{2,1,0:T(8,128)(2,1)S(1)}, u32[]{:S(2)}, u32[]{:S(2)}) async-start(bf16[32,256,128]{2,1,0:T(8,128)(2,1)} %copy-done), calls=%async_computation.1 | async-start | bytes 4194304 | tf_op jit(solution)/shard_map/all_to_all | solution.py:148
  40.8 0.0 copy-done.3
  40.8 7.8 %shard_map.77 = bf16[32,128,256]{2,1,0:T(8,128)(2,1)} custom-call(s32[32,8,128]{2,1,0:T(8,128)S(1)} %all_to_all.15.asked_ref, bf16[4,128,256]{2,1,0:T(8,128)(2,1)S(1)} %copy-done.3), custom_call_target="tpu_custom_call" | custom-call | bytes 5242880 | tf_op jit(solution)/shard_map/pallas_call | solution.py:15
  48.7 0.0 copy-start.5
  48.7 17.8 %all-to-all-done.1.panels_ref = bf16[32,256,128]{2,1,0:T(8,128)(2,1)S(1)} async-done(((bf16[32,256,128]{2,1,0:T(8,128)(2,1)}), bf16[32,256,128]{2,1,0:T(8,128)(2,1)S(1)}, u32[]{:S(2)}, u32[]{:S(2)}) %all-to-all-start.1) | async-done | bytes 2097184 | tf_op jit(solution)/shard_map/all_to_all | solution.py:148
  66.5 9.1 %all-to-all-start.2 = ((bf16[32,128,256]{2,1,0:T(8,128)(2,1)}), bf16[32,128,256]{2,1,0:T(8,128)(2,1)}, u32[]{:S(2)}, u32[]{:S(2)}) async-start(bf16[32,128,256]{2,1,0:T(8,128)(2,1)} %shard_map.77), calls=%async_computation.2 | async-start | bytes 4194304 | tf_op jit(solution)/shard_map/all_to_all | solution.py:148
  75.5 0.0 copy-done.5
  75.5 0.0 copy-done.7
  75.5 0.0 copy-done.8
  75.5 0.8 shard_map.73.hold_ref
  76.3 0.0 copy-done.1
  76.4 2.1 %shard_map.76 = (f32[48,128]{1,0:T(8,128)S(1)}, f32[48,128]{1,0:T(8,128)S(1)}, f32[48,128]{1,0:T(8,128)S(1)}, f32[48,128]{1,0:T(8,128)S(1)}) custom-call(s32[1]{0:T(128)} %bitcast.me_ref, s32[192,128]{1,0:T(8,128)S(1)} %shard_map.73.hold_ref, bf16[192,256]{1,0:T(8,128)(2,1)S(1)} %bitcast.16, bf16[32,256,128]{2,1,0:T(8,128)(2,1)S(1)} %all-to-all-done.1.panels_ref), custom_call_target="tpu_custom_call" | custom-call | flops 402653184 | bytes 3145728 | tf_op jit(solution)/shard_map/pallas_call | solution.py:15
  78.4 2.6 %collective-permute-start = (f32[48,128]{1,0:T(8,128)S(1)}, f32[48,128]{1,0:T(8,128)S(1)}, u32[]{:S(2)}, u32[]{:S(2)}) collective-permute-start(f32[48,128]{1,0:T(8,128)S(1)} %get-tuple-element.11), channel_id=1, source_target_pairs={{0,1},{1,2},{2,3},{3,4},{4,5},{5,6},{6,7},{7,8},{8,9},{9,10},{10,1... | collective-permute-start | bytes 73736 | tf_op jit(solution)/shard_map/ppermute | solution.py:101
  81.0 9.5 %collective-permute-start.1 = (f32[48,128]{1,0:T(8,128)S(1)}, f32[48,128]{1,0:T(8,128)S(1)}, u32[]{:S(2)}, u32[]{:S(2)}) collective-permute-start(f32[48,128]{1,0:T(8,128)S(1)} %get-tuple-element.12), channel_id=1, source_target_pairs={{0,15},{1,0},{2,1},{3,2},{4,3},{5,4},{6,5},{7,6},{8,7},{9,8},{10,9... | collective-permute-start | bytes 73736 | tf_op jit(solution)/shard_map/ppermute | solution.py:101
  90.5 4.4 %collective-permute-start.2 = (f32[48,128]{1,0:T(8,128)S(1)}, f32[48,128]{1,0:T(8,128)S(1)}, u32[]{:S(2)}, u32[]{:S(2)}) collective-permute-start(f32[48,128]{1,0:T(8,128)S(1)} %get-tuple-element.13), channel_id=1, source_target_pairs={{0,14},{1,15},{2,0},{3,1},{4,2},{5,3},{6,4},{7,5},{8,6},{9,7},{10,... | collective-permute-start | bytes 73736 | tf_op jit(solution)/shard_map/ppermute | solution.py:101
  94.9 0.0 collective-permute-done
  94.9 0.0 collective-permute-done.1
  95.0 2.2 %collective-permute-done.2 = f32[48,128]{1,0:T(8,128)S(1)} collective-permute-done((f32[48,128]{1,0:T(8,128)S(1)}, f32[48,128]{1,0:T(8,128)S(1)}, u32[]{:S(2)}, u32[]{:S(2)}) %collective-permute-start.2) | collective-permute-done | bytes 24608 | tf_op jit(solution)/shard_map/ppermute | solution.py:101
  97.2 9.5 %collective-permute-start.3 = (f32[48,128]{1,0:T(8,128)S(1)}, f32[48,128]{1,0:T(8,128)S(1)}, u32[]{:S(2)}, u32[]{:S(2)}) collective-permute-start(f32[48,128]{1,0:T(8,128)S(1)} %add_add_fusion.1), channel_id=1, source_target_pairs={{0,8},{1,9},{2,10},{3,11},{4,12},{5,13},{6,14},{7,15},{8,0},{9,1},... | collective-permute-start | bytes 73736 | tf_op jit(solution)/shard_map/ppermute | solution.py:101
  106.6 4.3 %collective-permute-start.4 = (f32[48,128]{1,0:T(8,128)S(1)}, f32[48,128]{1,0:T(8,128)S(1)}, u32[]{:S(2)}, u32[]{:S(2)}) collective-permute-start(f32[48,128]{1,0:T(8,128)S(1)} %add_add_fusion.1), channel_id=1, source_target_pairs={{0,4},{1,5},{2,6},{3,7},{4,8},{5,9},{6,10},{7,11},{8,12},{9,13},{1... | collective-permute-start | bytes 73736 | tf_op jit(solution)/shard_map/ppermute | solution.py:101
  111.0 5.4 %collective-permute-start.5 = (f32[48,128]{1,0:T(8,128)S(1)}, f32[48,128]{1,0:T(8,128)S(1)}, u32[]{:S(2)}, u32[]{:S(2)}) collective-permute-start(f32[48,128]{1,0:T(8,128)S(1)} %add_add_fusion.1), channel_id=1, source_target_pairs={{0,12},{1,13},{2,14},{3,15},{4,0},{5,1},{6,2},{7,3},{8,4},{9,5},{1... | collective-permute-start | bytes 73736 | tf_op jit(solution)/shard_map/ppermute | solution.py:101
  116.4 0.0 collective-permute-done.3
  116.4 0.0 collective-permute-done.4
  116.4 4.2 %collective-permute-done.5 = f32[48,128]{1,0:T(8,128)S(1)} collective-permute-done((f32[48,128]{1,0:T(8,128)S(1)}, f32[48,128]{1,0:T(8,128)S(1)}, u32[]{:S(2)}, u32[]{:S(2)}) %collective-permute-start.5) | collective-permute-done | bytes 24608 | tf_op jit(solution)/shard_map/ppermute | solution.py:101
  120.6 4.2 %collective-permute-start.6 = (f32[48,128]{1,0:T(8,128)S(1)}, f32[48,128]{1,0:T(8,128)S(1)}, u32[]{:S(2)}, u32[]{:S(2)}) collective-permute-start(f32[48,128]{1,0:T(8,128)S(1)} %add_add_fusion.refs_0_), channel_id=1, source_target_pairs={{0,15},{1,0},{2,1},{3,2},{4,3},{5,4},{6,5},{7,6},{8,7},{9,8},{10,9... | collective-permute-start | bytes 73736 | tf_op jit(solution)/shard_map/ppermute | solution.py:101
  124.8 1.9 %collective-permute-start.7 = (f32[48,128]{1,0:T(8,128)S(1)}, f32[48,128]{1,0:T(8,128)S(1)}, u32[]{:S(2)}, u32[]{:S(2)}) collective-permute-start(f32[48,128]{1,0:T(8,128)S(1)} %add_add_fusion.refs_0_), channel_id=1, source_target_pairs={{0,2},{1,3},{2,4},{3,5},{4,6},{5,7},{6,8},{7,9},{8,10},{9,11},{10,... | collective-permute-start | bytes 73736 | tf_op jit(solution)/shard_map/ppermute | solution.py:101
  126.7 3.6 %collective-permute-start.8 = (f32[48,128]{1,0:T(8,128)S(1)}, f32[48,128]{1,0:T(8,128)S(1)}, u32[]{:S(2)}, u32[]{:S(2)}) collective-permute-start(f32[48,128]{1,0:T(8,128)S(1)} %add_add_fusion.refs_0_), channel_id=1, source_target_pairs={{0,1},{1,2},{2,3},{3,4},{4,5},{5,6},{6,7},{7,8},{8,9},{9,10},{10,1... | collective-permute-start | bytes 73736 | tf_op jit(solution)/shard_map/ppermute | solution.py:101
  130.3 0.0 all-to-all-done.2.refs_4_
  130.3 0.0 collective-permute-done.6.refs_1_
  130.4 2.3 %collective-permute-done.7.refs_2_ = f32[48,128]{1,0:T(8,128)S(1)} collective-permute-done((f32[48,128]{1,0:T(8,128)S(1)}, f32[48,128]{1,0:T(8,128)S(1)}, u32[]{:S(2)}, u32[]{:S(2)}) %collective-permute-start.7) | collective-permute-done | bytes 24608 | tf_op jit(solution)/shard_map/ppermute | solution.py:101
  132.6 1.0 collective-permute-done.8.refs_3_
  133.6 0.9 copy-done.9
  134.6 4.5 %shard_map.78 = bf16[192,256]{1,0:T(8,128)(2,1)} custom-call(s32[1]{0:T(128)} %bitcast.me_ref, s32[192,128]{1,0:T(8,128)S(1)} %shard_map.73.hold_ref, f32[48,128]{1,0:T(8,128)S(1)} %add_add_fusion.refs_0_, f32[48,128]{1,0:T(8,128)S(1)} %collective-permute-done.6.refs_1_, f32[48,128]{1,0:T(8,128)S(1)} %collective-permute-done.7.refs_2_, ...), custom_call_target="tpu_custom_call" | custom-call | flops 805306368 | bytes 3145728 | tf_op jit(solution)/shard_map/pallas_call | solution.py:15
  (7 shorter events, 0.0 us)
Async XLA Ops:
  6.5 127.1 %reduce-scatter.2.cloned.1.call-start = ((), (), s32[]{:S(2)}) async-start(), calls=%async_computation.4 | async-start | bytes 3342336 | tf_op jit(solution)/shard_map/reduce_scatter | solution.py:135
  6.5 0.7 copy-start.4
  7.2 0.7 copy-start.6
  12.3 14.8 %copy-start.2 = (bf16[4,256,128]{2,1,0:T(8,128)(2,1)S(1)}, bf16[4,256,128]{2,1,0:T(8,128)(2,1)}, u32[]{:S(2)}) copy-start(bf16[4,256,128]{2,1,0:T(8,128)(2,1)} %store_ref.2) | copy-start | bytes 786436
  33.6 1.4 copy-start
  35.0 5.8 %copy-start.3 = (bf16[4,128,256]{2,1,0:T(8,128)(2,1)S(1)}, bf16[4,128,256]{2,1,0:T(8,128)(2,1)}, u32[]{:S(2)}) copy-start(bf16[4,128,256]{2,1,0:T(8,128)(2,1)} %store_ref.3) | copy-start | bytes 786436
  35.0 31.4 %all-to-all-start.1 = ((bf16[32,256,128]{2,1,0:T(8,128)(2,1)}), bf16[32,256,128]{2,1,0:T(8,128)(2,1)S(1)}, u32[]{:S(2)}, u32[]{:S(2)}) async-start(bf16[32,256,128]{2,1,0:T(8,128)(2,1)} %copy-done), calls=%async_computation.1 | async-start | bytes 4194304 | tf_op jit(solution)/shard_map/all_to_all | solution.py:148
  48.7 26.9 %copy-start.5 = (s32[1,16]{1,0:T(1,128)S(1)}, s32[1,16]{1,0:T(1,128)}, u32[]{:S(2)}) copy-start(s32[1,16]{1,0:T(1,128)} %refs_0_.3) | copy-start | bytes 196
  48.7 26.9 %copy-start.7 = (s32[128]{0:T(128)S(1)}, s32[128]{0:T(128)}, u32[]{:S(2)}) copy-start(s32[128]{0:T(128)} %refs_1_.3) | copy-start | bytes 1540
  48.7 26.9 %copy-start.8 = (s32[64]{0:T(128)S(1)}, s32[64]{0:T(128)}, u32[]{:S(2)}) copy-start(s32[64]{0:T(128)} %refs_2_.1) | copy-start | bytes 772
  48.7 27.7 %copy-start.1 = (bf16[3,64,256]{2,1,0:T(8,128)(2,1)S(1)}, bf16[3,64,256]{2,1,0:T(8,128)(2,1)}, u32[]{:S(2)}) copy-start(bf16[3,64,256]{2,1,0:T(8,128)(2,1)} %param.7) | copy-start | bytes 294916
  66.5 63.9 %all-to-all-start.2 = ((bf16[32,128,256]{2,1,0:T(8,128)(2,1)}), bf16[32,128,256]{2,1,0:T(8,128)(2,1)}, u32[]{:S(2)}, u32[]{:S(2)}) async-start(bf16[32,128,256]{2,1,0:T(8,128)(2,1)} %shard_map.77), calls=%async_computation.2 | async-start | bytes 4194304 | tf_op jit(solution)/shard_map/all_to_all | solution.py:148
  78.4 16.5 %collective-permute-start = (f32[48,128]{1,0:T(8,128)S(1)}, f32[48,128]{1,0:T(8,128)S(1)}, u32[]{:S(2)}, u32[]{:S(2)}) collective-permute-start(f32[48,128]{1,0:T(8,128)S(1)} %get-tuple-element.11), channel_id=1, source_target_pairs={{0,1},{1,2},{2,3},{3,4},{4,5},{5,6},{6,7},{7,8},{8,9},{9,10},{10,1... | collective-permute-start | bytes 73736 | tf_op jit(solution)/shard_map/ppermute | solution.py:101
  81.0 13.9 %collective-permute-start.1 = (f32[48,128]{1,0:T(8,128)S(1)}, f32[48,128]{1,0:T(8,128)S(1)}, u32[]{:S(2)}, u32[]{:S(2)}) collective-permute-start(f32[48,128]{1,0:T(8,128)S(1)} %get-tuple-element.12), channel_id=1, source_target_pairs={{0,15},{1,0},{2,1},{3,2},{4,3},{5,4},{6,5},{7,6},{8,7},{9,8},{10,9... | collective-permute-start | bytes 73736 | tf_op jit(solution)/shard_map/ppermute | solution.py:101
  90.5 6.6 %collective-permute-start.2 = (f32[48,128]{1,0:T(8,128)S(1)}, f32[48,128]{1,0:T(8,128)S(1)}, u32[]{:S(2)}, u32[]{:S(2)}) collective-permute-start(f32[48,128]{1,0:T(8,128)S(1)} %get-tuple-element.13), channel_id=1, source_target_pairs={{0,14},{1,15},{2,0},{3,1},{4,2},{5,3},{6,4},{7,5},{8,6},{9,7},{10,... | collective-permute-start | bytes 73736 | tf_op jit(solution)/shard_map/ppermute | solution.py:101
  97.2 19.2 %collective-permute-start.3 = (f32[48,128]{1,0:T(8,128)S(1)}, f32[48,128]{1,0:T(8,128)S(1)}, u32[]{:S(2)}, u32[]{:S(2)}) collective-permute-start(f32[48,128]{1,0:T(8,128)S(1)} %add_add_fusion.1), channel_id=1, source_target_pairs={{0,8},{1,9},{2,10},{3,11},{4,12},{5,13},{6,14},{7,15},{8,0},{9,1},... | collective-permute-start | bytes 73736 | tf_op jit(solution)/shard_map/ppermute | solution.py:101
  106.6 9.8 %collective-permute-start.4 = (f32[48,128]{1,0:T(8,128)S(1)}, f32[48,128]{1,0:T(8,128)S(1)}, u32[]{:S(2)}, u32[]{:S(2)}) collective-permute-start(f32[48,128]{1,0:T(8,128)S(1)} %add_add_fusion.1), channel_id=1, source_target_pairs={{0,4},{1,5},{2,6},{3,7},{4,8},{5,9},{6,10},{7,11},{8,12},{9,13},{1... | collective-permute-start | bytes 73736 | tf_op jit(solution)/shard_map/ppermute | solution.py:101
  111.0 9.6 %collective-permute-start.5 = (f32[48,128]{1,0:T(8,128)S(1)}, f32[48,128]{1,0:T(8,128)S(1)}, u32[]{:S(2)}, u32[]{:S(2)}) collective-permute-start(f32[48,128]{1,0:T(8,128)S(1)} %add_add_fusion.1), channel_id=1, source_target_pairs={{0,12},{1,13},{2,14},{3,15},{4,0},{5,1},{6,2},{7,3},{8,4},{9,5},{1... | collective-permute-start | bytes 73736 | tf_op jit(solution)/shard_map/ppermute | solution.py:101
  120.6 9.8 %collective-permute-start.6 = (f32[48,128]{1,0:T(8,128)S(1)}, f32[48,128]{1,0:T(8,128)S(1)}, u32[]{:S(2)}, u32[]{:S(2)}) collective-permute-start(f32[48,128]{1,0:T(8,128)S(1)} %add_add_fusion.refs_0_), channel_id=1, source_target_pairs={{0,15},{1,0},{2,1},{3,2},{4,3},{5,4},{6,5},{7,6},{8,7},{9,8},{10,9... | collective-permute-start | bytes 73736 | tf_op jit(solution)/shard_map/ppermute | solution.py:101
  124.8 7.8 %collective-permute-start.7 = (f32[48,128]{1,0:T(8,128)S(1)}, f32[48,128]{1,0:T(8,128)S(1)}, u32[]{:S(2)}, u32[]{:S(2)}) collective-permute-start(f32[48,128]{1,0:T(8,128)S(1)} %add_add_fusion.refs_0_), channel_id=1, source_target_pairs={{0,2},{1,3},{2,4},{3,5},{4,6},{5,7},{6,8},{7,9},{8,10},{9,11},{10,... | collective-permute-start | bytes 73736 | tf_op jit(solution)/shard_map/ppermute | solution.py:101
  126.7 6.9 %collective-permute-start.8 = (f32[48,128]{1,0:T(8,128)S(1)}, f32[48,128]{1,0:T(8,128)S(1)}, u32[]{:S(2)}, u32[]{:S(2)}) collective-permute-start(f32[48,128]{1,0:T(8,128)S(1)} %add_add_fusion.refs_0_), channel_id=1, source_target_pairs={{0,1},{1,2},{2,3},{3,4},{4,5},{5,6},{6,7},{7,8},{8,9},{9,10},{10,1... | collective-permute-start | bytes 73736 | tf_op jit(solution)/shard_map/ppermute | solution.py:101
  133.6 0.9 copy-start.9
Sparse Core Ops, SparseCore 0:
  12.5 81.2 reduce-scatter.1

commit v2 on v1

v2 whole, which is shorter than its diff:
```python
import jax
import jax.numpy as jnp
from jax import lax
from jax.experimental import pallas as pl
from jax.experimental.pallas import tpu as pltpu
from jax.sharding import PartitionSpec as P

MIB = 1024 * 1024
SMEM, VMEM, HBM = (pl.BlockSpec(memory_space=m) for m in (pltpu.SMEM, pltpu.VMEM, pltpu.HBM))
DMA = pltpu.SemaphoreType.DMA
MOST_CHUNKS = 8
ALL = 60


def local_call(body, outs, flops, moved, in_specs, out_specs, scratch, operands, grid=(), limit=16):
    return pl.pallas_call(
        body,
        out_shape=outs,
        grid=grid,
        in_specs=in_specs,
        out_specs=out_specs,
        scratch_shapes=scratch,
        compiler_params=pltpu.CompilerParams(vmem_limit_bytes=limit * MIB),
        cost_estimate=pl.CostEstimate(flops=flops, bytes_accessed=moved, transcendentals=0),
    )(*operands)


def wish_kernel(stored, list_ref, place_ref, wish_ref):
    wish_ref[...] = jnp.zeros_like(wish_ref)
    for s in range(list_ref.shape[1]):
        position = place_ref[list_ref[0, s]]
        slot = lax.rem(position, stored)
        wish_ref[lax.div(position, stored)] = jnp.full(wish_ref.shape[1:], slot, jnp.int32)


def base_kernel(x_ref, weight_ref, out_ref):
    x = x_ref[...]
    width = out_ref.shape[2]
    for c in range(out_ref.shape[0]):
        out_ref[c] = jnp.dot(
            x, weight_ref[:, c * width:(c + 1) * width], preferred_element_type=jnp.float32
        )


def pick(asked_ref, store_ref, out_ref, sems):
    def copy(q):
        return pltpu.make_async_copy(
            store_ref.at[asked_ref[q, 0, 0]], out_ref.at[q], sems.at[q]
        )

    count = out_ref.shape[0]
    pl.loop(0, count)(lambda q: copy(q).start())
    return lambda: pl.loop(0, count)(lambda q: copy(q).wait())


def pick_kernel(asked_ref, store_ref, out_ref, sems):
    pick(asked_ref, store_ref, out_ref, sems)()


def pick_hold_kernel(stored, steps, asked_ref, list_ref, place_ref, slot_ref, store_ref,
                     out_ref, hold_ref, sems):
    finish = pick(asked_ref, store_ref, out_ref, sems)
    requests = slot_ref.shape[0]

    @pl.loop(0, requests, unroll=8)
    def _(r):
        holder = lax.div(place_ref[list_ref[0, slot_ref[r]]], stored)
        for step in range(steps):
            hold_ref[pl.ds(step * requests + r, 1), :] = jnp.full((1, 128), holder, jnp.int32)

    finish()


def shrink_kernel(hold_ref, x_ref, panels_ref, out_ref):
    hold = hold_ref[...]
    x = x_ref[...]
    out_ref[...] = jnp.zeros_like(out_ref)

    @pl.loop(0, panels_ref.shape[0], unroll=4)
    def _(q):
        product = jnp.dot(x, panels_ref[q], preferred_element_type=jnp.float32)
        out_ref[...] = jnp.where(hold == q, product, out_ref[...])


def final_kernel(hold_ref, shrink_ref, other_ref, panels_hbm, base_hbm, out_ref,
                 total_ref, panels_ref, base_ref, sems):
    chunks = sems.shape[0] - 1
    each = panels_ref.shape[0] // chunks

    def copy(c):
        part = pl.ds(c * each, each)
        return pltpu.make_async_copy(panels_hbm.at[part], panels_ref.at[part], sems.at[c])

    base_copy = pltpu.make_async_copy(base_hbm, base_ref, sems.at[chunks])
    for c in range(chunks):
        copy(c).start()
    base_copy.start()

    hold = hold_ref[...]
    hold = jnp.concatenate([hold] * (total_ref.shape[1] // hold.shape[1]), axis=1)
    shrink = shrink_ref[...] + other_ref[...]
    high = shrink.astype(jnp.bfloat16)
    low = (shrink - high.astype(jnp.float32)).astype(jnp.bfloat16)
    both = jnp.concatenate([high, low], axis=1)
    total_ref[...] = jnp.zeros_like(total_ref)

    for c in range(chunks):
        copy(c).wait()
        for q in range(c * each, (c + 1) * each):
            panel = panels_ref[q]
            product = jnp.dot(
                both, jnp.concatenate([panel, panel], axis=0), preferred_element_type=jnp.float32
            )
            total_ref[...] = jnp.where(hold == q, product, total_ref[...])

    base_copy.wait()
    out_ref[...] = (base_ref[...] + total_ref[...]).astype(out_ref.dtype)


def across(value, bit, size):
    return lax.ppermute(value, "tensor", [(i, i ^ bit) for i in range(size)])


def on_device(attn_out, base_weight, store_a, store_b, adapter_lists, placement_map, request_slot):
    replicas = lax.axis_size("dp")
    columns = lax.axis_size("tensor")
    stored, depth, rank = store_a.shape
    steps, requests, _ = attn_out.shape
    width = store_b.shape[2]
    rows = steps * requests
    f32, bf16, i32 = jnp.float32, jnp.bfloat16, jnp.int32
    shaped = jax.ShapeDtypeStruct
    x = attn_out.reshape(rows, depth)

    wish = local_call(
        lambda *refs: wish_kernel(stored, *refs), shaped((replicas, 1, 128), i32), 0, 1 << 14,
        [SMEM, SMEM], VMEM, [], (adapter_lists, placement_map),
    )
    asked = lax.all_to_all(wish, "dp", split_axis=0, concat_axis=0, tiled=True)

    partial = local_call(
        base_kernel, shaped((columns, rows, width), f32),
        2 * rows * depth * columns * width, 5 << 20,
        [pl.BlockSpec((rows, depth), lambda i: (0, 0)),
         pl.BlockSpec((depth, 4 * width), lambda i: (0, i))],
        pl.BlockSpec((4, rows, width), lambda i: (i, 0, 0)), [], (x, base_weight),
        grid=(columns // 4,), limit=ALL,
    )
    base = lax.psum_scatter(partial, "tensor", scatter_dimension=0, tiled=True)[0]

    picked_a = local_call(
        pick_kernel, shaped((replicas,) + store_a.shape[1:], bf16), 0, 4 << 20,
        [SMEM, VMEM], HBM, [DMA((replicas,))], (asked, store_a), limit=ALL,
    )
    got_a = lax.all_to_all(picked_a, "dp", split_axis=0, concat_axis=0, tiled=True)
    picked_b, hold = local_call(
        lambda *refs: pick_hold_kernel(stored, steps, *refs),
        (shaped((replicas,) + store_b.shape[1:], bf16), shaped((rows, 128), i32)), 0, 4 << 20,
        [SMEM, SMEM, SMEM, SMEM, VMEM], (HBM, VMEM), [DMA((replicas,))],
        (asked, adapter_lists, placement_map, request_slot, store_b),
    )
    got_b = lax.all_to_all(picked_b, "dp", split_axis=0, concat_axis=0, tiled=True)

    shrink = local_call(
        shrink_kernel, shaped((rows, rank), f32), 2 * rows * replicas * depth * rank, 3 << 20,
        [VMEM] * 3, VMEM, [], (hold, x, got_a),
    )
    bit = columns // 2
    while bit > 1:
        shrink = shrink + across(shrink, bit, columns)
        bit //= 2
    out = local_call(
        final_kernel, shaped((rows, width), bf16),
        4 * rows * replicas * rank * width, 3 << 20,
        [VMEM, VMEM, VMEM, HBM, HBM], VMEM,
        [pltpu.VMEM((rows, width), f32), pltpu.VMEM(got_b.shape, bf16),
         pltpu.VMEM((rows, width), f32), DMA((min(MOST_CHUNKS, replicas) + 1,))],
        (hold, shrink, across(shrink, 1, columns), got_b, base), limit=40,
    )
    return out.reshape(steps, requests, width)


def solution(mesh):
    placed = (
        P(None, "dp", "tensor"),
        P("tensor", None),
        P("dp", "tensor", None),
        P("dp", None, "tensor"),
        P("dp", None),
        P(),
        P("dp"),
    )
    return jax.shard_map(
        on_device, mesh=mesh, in_specs=placed, out_specs=P(None, "dp", "tensor"), check_vma=False
    )
```

time: 147 us -> 136 us (0.925)
  starting transfers between devices: 60.2 us -> 51 us
  waiting for transfers between devices: 27.5 us -> 34.3 us
  Pallas kernels: 22.3 us -> 18.1 us
  matrix products: 3.87 us -> 0 us
    ppermute x9 -> x4, starting transfers between devices: 45.4 us -> 35.9 us  [across(): return lax.ppermute(value, 'tensor', [(i, i ^ bit) for i in range(size)])]
    ppermute x9 -> x4, waiting for transfers between devices: 9.67 us -> 14.6 us  [across(): return lax.ppermute(value, 'tensor', [(i, i ^ bit) for i in range(size)])]
    pallas_call x6, Pallas kernels: 22.3 us -> 18.1 us  [local_call(): pl.pallas_call(body, out_shape=outs, grid=grid, in_specs=in_specs, out_sp...]
    dot_general x1 -> x0, matrix products: 3.87 us -> none  [on_device(): jnp.einsum('icw,ri->crw', base_weight.reshape(depth, columns, width), x_l...]
    all_to_all x2, waiting for transfers between devices: 17.8 us -> 19.7 us  [the longest x1 19.7 us: on_device(): lax.all_to_all(picked_a, 'dp', split_axis=0, concat_axis=0, tiled=True)]
    unnamed x20 -> x16, local copies, waits for them, and re-layouts: 3.64 us -> 2.95 us
  transfers between devices with their start and end apart: 12 -> 7, of which waited for: 5 -> 5; matrix products, arithmetic and copies ran while one was open for 0% -> 0% of each run, Pallas kernels for 12% -> 7%
where the time goes in v2:
time: 136 us; the launch traced here: 135 us
  starting transfers between devices  51 us (38%)
  waiting for transfers between devices  34.3 us (25%)
  Pallas kernels  18.1 us (13%)
  blocking collectives  14.7 us (11%)
  between operations  13.6 us (10%)
  local copies, waits for them, and re-layouts  2.95 us (2%)
    ppermute x4, starting transfers between devices, across(): return lax.ppermute(value, 'tensor', [(i, i ^ bit) for i in range(size)])  35.9 us
    all_to_all x1, waiting for transfers between devices, on_device(): lax.all_to_all(picked_a, 'dp', split_axis=0, concat_axis=0, tiled=True)  19.7 us
    pallas_call x6, Pallas kernels, local_call(): pl.pallas_call(body, out_shape=outs, grid=grid, in_specs=in_specs, out_sp...  18.1 us
    all_to_all x1, blocking collectives, on_device(): asked = lax.all_to_all(wish, 'dp', split_axis=0, concat_axis=0, tiled=True)  14.7 us
    ppermute x4, waiting for transfers between devices, across(): return lax.ppermute(value, 'tensor', [(i, i ^ bit) for i in range(size)])  14.6 us
    all_to_all x1, starting transfers between devices, on_device(): lax.all_to_all(picked_b, 'dp', split_axis=0, concat_axis=0, tiled=True)  9.18 us
    all_to_all x1, starting transfers between devices, on_device(): lax.all_to_all(picked_a, 'dp', split_axis=0, concat_axis=0, tiled=True)  5.91 us
    unnamed x16, local copies, waits for them, and re-layouts  2.95 us
  transfers between devices with their start and end apart: 7, of which 5 were waited for; matrix products, arithmetic and copies ran while one was open for 0% of the time, Pallas kernels for 7%

profile of v2, /device:TPU:6, one launch (start us, length us, event | category | flops | bytes accessed | tf_op | source)
XLA Modules:
  0.0 134.7 jit_solution(6524095877303861406)
XLA Ops:
  6.5 0.0 reduce-scatter.2.cloned.1.call-start
  6.5 4.4 %shard_map.77 = f32[16,192,256]{2,1,0:T(8,128)} custom-call(bf16[192,256]{1,0:T(8,128)(2,1)} %bitcast.3, bf16[256,4096]{1,0:T(8,128)(2,1)} %weight_ref.1), custom_call_target="tpu_custom_call" | custom-call | flops 402653184 | bytes 5242880 | tf_op jit(solution)/shard_map/pallas_call | solution.py:16
  11.0 0.0 copy-start.4
  11.0 0.0 copy-start.5
  11.0 0.0 reduce-scatter.2.cloned.1.call-update
  11.0 0.6 copy-done.4
  11.6 0.0 copy-done.5
  11.7 0.6 shard_map.73
  12.3 14.7 %all_to_all.15.refs_0_.asked_ref = s32[32,1,128]{2,1,0:T(1,128)} all-to-all(s32[32,1,128]{2,1,0:T(1,128)S(1)} %shard_map.73), channel_id=1, replica_groups=mesh['dp'=32,'tensor'=16] {'dp'}, dimensions={0} | all-to-all | bytes 32768 | tf_op jit(solution)/shard_map/all_to_all | solution.py:139
  27.0 2.6 %shard_map.75 = bf16[32,256,128]{2,1,0:T(8,128)(2,1)} custom-call(s32[32,1,128]{2,1,0:T(1,128)} %all_to_all.15.refs_0_.asked_ref, bf16[4,256,128]{2,1,0:T(8,128)(2,1)} %store_ref.1), custom_call_target="tpu_custom_call" | custom-call | bytes 4194304 | tf_op jit(solution)/shard_map/pallas_call | solution.py:16
  29.6 0.0 copy-start.2
  29.6 0.0 copy-start.3
  29.6 0.0 copy-start.6
  29.6 5.9 %all-to-all-start.1 = ((bf16[32,256,128]{2,1,0:T(8,128)(2,1)}), bf16[32,256,128]{2,1,0:T(8,128)(2,1)S(1)}, u32[]{:S(2)}, u32[]{:S(2)}) async-start(bf16[32,256,128]{2,1,0:T(8,128)(2,1)} %shard_map.75), calls=%async_computation.1 | async-start | bytes 4194304 | tf_op jit(solution)/shard_map/all_to_all | solution.py:155
  35.6 0.0 copy-done.2
  35.6 0.0 copy-done.3
  35.6 0.0 copy-done.6
  35.6 4.5 %shard_map.74 = (bf16[32,128,256]{2,1,0:T(8,128)(2,1)S(1)}, s32[192,128]{1,0:T(8,128)S(1)}) custom-call(s32[32,1,128]{2,1,0:T(1,128)S(1)} %copy-done.3, s32[1,16]{1,0:T(1,128)S(1)} %copy-done.4, s32[128]{0:T(128)S(1)} %copy-done.5, s32[64]{0:T(128)S(1)} %copy-done.6, bf16[4,128,256]{2,1,0:T(8,128)(2,1)S(1)} %copy-done.2), custom_call_target="tpu_custom_call" | custom-call | bytes 4194304 | tf_op jit(solution)/shard_map/pallas_call | solution.py:16
  40.1 0.0 copy-start
  40.1 1.4 %copy-done = bf16[32,128,256]{2,1,0:T(8,128)(2,1)} copy-done((bf16[32,128,256]{2,1,0:T(8,128)(2,1)}, bf16[32,128,256]{2,1,0:T(8,128)(2,1)S(1)}, u32[]{:S(2)}) %copy-start) | copy-done | bytes 2097176
  41.5 19.7 %all-to-all-done.1.panels_ref = bf16[32,256,128]{2,1,0:T(8,128)(2,1)S(1)} async-done(((bf16[32,256,128]{2,1,0:T(8,128)(2,1)}), bf16[32,256,128]{2,1,0:T(8,128)(2,1)S(1)}, u32[]{:S(2)}, u32[]{:S(2)}) %all-to-all-start.1) | async-done | bytes 2097184 | tf_op jit(solution)/shard_map/all_to_all | solution.py:155
  61.2 0.0 copy-start.1
  61.2 9.2 %all-to-all-start.2 = ((bf16[32,128,256]{2,1,0:T(8,128)(2,1)}), bf16[32,128,256]{2,1,0:T(8,128)(2,1)}, u32[]{:S(2)}, u32[]{:S(2)}) async-start(bf16[32,128,256]{2,1,0:T(8,128)(2,1)} %copy-done), calls=%async_computation.2 | async-start | bytes 4194304 | tf_op jit(solution)/shard_map/all_to_all | solution.py:162
  70.4 0.0 copy-done.1
  70.4 2.1 %shard_map.76 = f32[192,128]{1,0:T(8,128)S(1)} custom-call(s32[192,128]{1,0:T(8,128)S(1)} %get-tuple-element.7.hold_ref, bf16[192,256]{1,0:T(8,128)(2,1)S(1)} %bitcast.4, bf16[32,256,128]{2,1,0:T(8,128)(2,1)S(1)} %all-to-all-done.1.panels_ref), custom_call_target="tpu_custom_call" | custom-call | flops 402653184 | bytes 3145728 | tf_op jit(solution)/shard_map/pallas_call | solution.py:16
  72.5 14.0 %collective-permute-start = (f32[192,128]{1,0:T(8,128)S(1)}, f32[192,128]{1,0:T(8,128)S(1)}, u32[]{:S(2)}, u32[]{:S(2)}) collective-permute-start(f32[192,128]{1,0:T(8,128)S(1)} %shard_map.76), channel_id=1, source_target_pairs={{0,8},{1,9},{2,10},{3,11},{4,12},{5,13},{6,14},{7,15},{8,0},{9,1},... | collective-permute-start | bytes 294920 | tf_op jit(solution)/shard_map/ppermute | solution.py:121
  86.5 6.8 %collective-permute-done = f32[192,128]{1,0:T(8,128)S(1)} collective-permute-done((f32[192,128]{1,0:T(8,128)S(1)}, f32[192,128]{1,0:T(8,128)S(1)}, u32[]{:S(2)}, u32[]{:S(2)}) %collective-permute-start) | collective-permute-done | bytes 98336 | tf_op jit(solution)/shard_map/ppermute | solution.py:121
  93.2 8.7 %collective-permute-start.1 = (f32[192,128]{1,0:T(8,128)S(1)}, f32[192,128]{1,0:T(8,128)S(1)}, u32[]{:S(2)}, u32[]{:S(2)}) collective-permute-start(f32[192,128]{1,0:T(8,128)S(1)} %add.11), channel_id=1, source_target_pairs={{0,4},{1,5},{2,6},{3,7},{4,0},{5,1},{6,2},{7,3},{8,12},{9,13},{10,... | collective-permute-start | bytes 294920 | tf_op jit(solution)/shard_map/ppermute | solution.py:121
  101.9 2.6 %collective-permute-done.1 = f32[192,128]{1,0:T(8,128)S(1)} collective-permute-done((f32[192,128]{1,0:T(8,128)S(1)}, f32[192,128]{1,0:T(8,128)S(1)}, u32[]{:S(2)}, u32[]{:S(2)}) %collective-permute-start.1) | collective-permute-done | bytes 98336 | tf_op jit(solution)/shard_map/ppermute | solution.py:121
  104.5 7.0 %collective-permute-start.2 = (f32[192,128]{1,0:T(8,128)S(1)}, f32[192,128]{1,0:T(8,128)S(1)}, u32[]{:S(2)}, u32[]{:S(2)}) collective-permute-start(f32[192,128]{1,0:T(8,128)S(1)} %add.12), channel_id=1, source_target_pairs={{0,2},{1,3},{2,0},{3,1},{4,6},{5,7},{6,4},{7,5},{8,10},{9,11},{10,... | collective-permute-start | bytes 294920 | tf_op jit(solution)/shard_map/ppermute | solution.py:121
  111.5 2.7 %collective-permute-done.2 = f32[192,128]{1,0:T(8,128)S(1)} collective-permute-done((f32[192,128]{1,0:T(8,128)S(1)}, f32[192,128]{1,0:T(8,128)S(1)}, u32[]{:S(2)}, u32[]{:S(2)}) %collective-permute-start.2) | collective-permute-done | bytes 98336 | tf_op jit(solution)/shard_map/ppermute | solution.py:121
  114.2 6.3 %collective-permute-start.3 = (f32[192,128]{1,0:T(8,128)S(1)}, f32[192,128]{1,0:T(8,128)S(1)}, u32[]{:S(2)}, u32[]{:S(2)}) collective-permute-start(f32[192,128]{1,0:T(8,128)S(1)} %add.13.shrink_ref), channel_id=1, source_target_pairs={{0,1},{1,0},{2,3},{3,2},{4,5},{5,4},{6,7},{7,6},{8,9},{9,8},{10,11... | collective-permute-start | bytes 294920 | tf_op jit(solution)/shard_map/ppermute | solution.py:121
  120.5 0.0 all-to-all-done.2.panels_hbm
  120.5 2.6 %collective-permute-done.3.other_ref = f32[192,128]{1,0:T(8,128)S(1)} collective-permute-done((f32[192,128]{1,0:T(8,128)S(1)}, f32[192,128]{1,0:T(8,128)S(1)}, u32[]{:S(2)}, u32[]{:S(2)}) %collective-permute-start.3) | collective-permute-done | bytes 98336 | tf_op jit(solution)/shard_map/ppermute | solution.py:121
  123.1 0.0 reduce-scatter.2.cloned.1.call-done
  123.1 0.0 copy-start.7
  123.1 0.9 copy-done.7
  124.0 3.9 %shard_map.78 = bf16[192,256]{1,0:T(8,128)(2,1)} custom-call(s32[192,128]{1,0:T(8,128)S(1)} %get-tuple-element.7.hold_ref, f32[192,128]{1,0:T(8,128)S(1)} %add.13.shrink_ref, f32[192,128]{1,0:T(8,128)S(1)} %collective-permute-done.3.other_ref, bf16[32,128,256]{2,1,0:T(8,128)(2,1)} %all-to-all-done.2.panels_hbm, f32[192,256]{1,0:T(8,128)S(1)} %bitcast.5), custom_call_target="tpu_custom_call" | custom-call | flops 805306368 | bytes 3145728 | tf_op jit(solution)/shard_map/pallas_call | solution.py:16
  (3 shorter events, 0.0 us)
Async XLA Ops:
  6.5 116.6 %reduce-scatter.2.cloned.1.call-start = ((), (), s32[]{:S(2)}) async-start(), calls=%async_computation.4 | async-start | bytes 3342336 | tf_op jit(solution)/shard_map/reduce_scatter | solution.py:149
  11.0 0.7 copy-start.4
  11.0 0.7 copy-start.5
  29.6 5.9 %copy-start.2 = (bf16[4,128,256]{2,1,0:T(8,128)(2,1)S(1)}, bf16[4,128,256]{2,1,0:T(8,128)(2,1)}, u32[]{:S(2)}) copy-start(bf16[4,128,256]{2,1,0:T(8,128)(2,1)} %refs_4_.1) | copy-start | bytes 786436
  29.6 5.9 %copy-start.3 = (s32[32,1,128]{2,1,0:T(1,128)S(1)}, s32[32,1,128]{2,1,0:T(1,128)}, u32[]{:S(2)}) copy-start(s32[32,1,128]{2,1,0:T(1,128)} %all_to_all.15.refs_0_.asked_ref) | copy-start | bytes 49156
  29.6 5.9 %copy-start.6 = (s32[64]{0:T(128)S(1)}, s32[64]{0:T(128)}, u32[]{:S(2)}) copy-start(s32[64]{0:T(128)} %refs_3_.1) | copy-start | bytes 772
  29.6 31.5 %all-to-all-start.1 = ((bf16[32,256,128]{2,1,0:T(8,128)(2,1)}), bf16[32,256,128]{2,1,0:T(8,128)(2,1)S(1)}, u32[]{:S(2)}, u32[]{:S(2)}) async-start(bf16[32,256,128]{2,1,0:T(8,128)(2,1)} %shard_map.75), calls=%async_computation.1 | async-start | bytes 4194304 | tf_op jit(solution)/shard_map/all_to_all | solution.py:155
  40.1 1.4 %copy-start = (bf16[32,128,256]{2,1,0:T(8,128)(2,1)}, bf16[32,128,256]{2,1,0:T(8,128)(2,1)S(1)}, u32[]{:S(2)}) copy-start(bf16[32,128,256]{2,1,0:T(8,128)(2,1)S(1)} %get-tuple-element.8) | copy-start | bytes 6291460
  61.2 9.2 %copy-start.1 = (bf16[3,64,256]{2,1,0:T(8,128)(2,1)S(1)}, bf16[3,64,256]{2,1,0:T(8,128)(2,1)}, u32[]{:S(2)}) copy-start(bf16[3,64,256]{2,1,0:T(8,128)(2,1)} %param.7) | copy-start | bytes 294916
  61.2 59.3 %all-to-all-start.2 = ((bf16[32,128,256]{2,1,0:T(8,128)(2,1)}), bf16[32,128,256]{2,1,0:T(8,128)(2,1)}, u32[]{:S(2)}, u32[]{:S(2)}) async-start(bf16[32,128,256]{2,1,0:T(8,128)(2,1)} %copy-done), calls=%async_computation.2 | async-start | bytes 4194304 | tf_op jit(solution)/shard_map/all_to_all | solution.py:162
  72.5 20.8 %collective-permute-start = (f32[192,128]{1,0:T(8,128)S(1)}, f32[192,128]{1,0:T(8,128)S(1)}, u32[]{:S(2)}, u32[]{:S(2)}) collective-permute-start(f32[192,128]{1,0:T(8,128)S(1)} %shard_map.76), channel_id=1, source_target_pairs={{0,8},{1,9},{2,10},{3,11},{4,12},{5,13},{6,14},{7,15},{8,0},{9,1},... | collective-permute-start | bytes 294920 | tf_op jit(solution)/shard_map/ppermute | solution.py:121
  93.2 11.2 %collective-permute-start.1 = (f32[192,128]{1,0:T(8,128)S(1)}, f32[192,128]{1,0:T(8,128)S(1)}, u32[]{:S(2)}, u32[]{:S(2)}) collective-permute-start(f32[192,128]{1,0:T(8,128)S(1)} %add.11), channel_id=1, source_target_pairs={{0,4},{1,5},{2,6},{3,7},{4,0},{5,1},{6,2},{7,3},{8,12},{9,13},{10,... | collective-permute-start | bytes 294920 | tf_op jit(solution)/shard_map/ppermute | solution.py:121
  104.5 9.7 %collective-permute-start.2 = (f32[192,128]{1,0:T(8,128)S(1)}, f32[192,128]{1,0:T(8,128)S(1)}, u32[]{:S(2)}, u32[]{:S(2)}) collective-permute-start(f32[192,128]{1,0:T(8,128)S(1)} %add.12), channel_id=1, source_target_pairs={{0,2},{1,3},{2,0},{3,1},{4,6},{5,7},{6,4},{7,5},{8,10},{9,11},{10,... | collective-permute-start | bytes 294920 | tf_op jit(solution)/shard_map/ppermute | solution.py:121
  114.2 8.9 %collective-permute-start.3 = (f32[192,128]{1,0:T(8,128)S(1)}, f32[192,128]{1,0:T(8,128)S(1)}, u32[]{:S(2)}, u32[]{:S(2)}) collective-permute-start(f32[192,128]{1,0:T(8,128)S(1)} %add.13.shrink_ref), channel_id=1, source_target_pairs={{0,1},{1,0},{2,3},{3,2},{4,5},{5,4},{6,7},{7,6},{8,9},{9,8},{10,11... | collective-permute-start | bytes 294920 | tf_op jit(solution)/shard_map/ppermute | solution.py:121
  123.1 0.9 copy-start.7
Sparse Core Ops, SparseCore 0:
  11.1 87.9 reduce-scatter.1

commit v3 on v2

--- a/solution.py
+++ b/solution.py
@@ -9,6 +9,8 @@
 SMEM, VMEM, HBM = (pl.BlockSpec(memory_space=m) for m in (pltpu.SMEM, pltpu.VMEM, pltpu.HBM))
 DMA = pltpu.SemaphoreType.DMA
 MOST_CHUNKS = 8
+ADD_LONG = 2 * 10**10
+LONG = 2275 * 10**7
 ALL = 60
 
 
@@ -71,19 +73,34 @@
     finish()
 
 
-def shrink_kernel(hold_ref, x_ref, panels_ref, out_ref):
+def shrink_kernel(me_ref, hold_ref, x_ref, panels_ref, mine_ref, other_ref, total_ref):
     hold = hold_ref[...]
     x = x_ref[...]
-    out_ref[...] = jnp.zeros_like(out_ref)
+    total_ref[...] = jnp.zeros_like(total_ref)
 
     @pl.loop(0, panels_ref.shape[0], unroll=4)
     def _(q):
         product = jnp.dot(x, panels_ref[q], preferred_element_type=jnp.float32)
-        out_ref[...] = jnp.where(hold == q, product, out_ref[...])
-
-
-def final_kernel(hold_ref, shrink_ref, other_ref, panels_hbm, base_hbm, out_ref,
-                 total_ref, panels_ref, base_ref, sems):
+        total_ref[...] = jnp.where(hold == q, product, total_ref[...])
+
+    mine, other = halves(me_ref, total_ref)
+    mine_ref[...] = total_ref[mine, :]
+    other_ref[...] = total_ref[other, :]
+
+
+def add_kernel(a_ref, b_ref, out_ref):
+    out_ref[...] = a_ref[...] + b_ref[...]
+
+
+def halves(me_ref, ref):
+    half = ref.shape[0] // 2
+    odd = lax.rem(me_ref[0], 2)
+    return (pl.ds(pl.multiple_of(odd * half, half), half),
+            pl.ds(pl.multiple_of((1 - odd) * half, half), half))
+
+
+def final_kernel(me_ref, hold_ref, mine_ref, other_ref, panels_hbm, base_hbm, out_ref,
+                 shrink_ref, total_ref, panels_ref, base_ref, sems):
     chunks = sems.shape[0] - 1
     each = panels_ref.shape[0] // chunks
 
@@ -98,7 +115,10 @@
 
     hold = hold_ref[...]
     hold = jnp.concatenate([hold] * (total_ref.shape[1] // hold.shape[1]), axis=1)
-    shrink = shrink_ref[...] + other_ref[...]
+    mine, other = halves(me_ref, shrink_ref)
+    shrink_ref[mine, :] = mine_ref[...]
+    shrink_ref[other, :] = other_ref[...]
+    shrink = shrink_ref[...]
     high = shrink.astype(jnp.bfloat16)
     low = (shrink - high.astype(jnp.float32)).astype(jnp.bfloat16)
     both = jnp.concatenate([high, low], axis=1)
@@ -148,6 +168,7 @@
     )
     base = lax.psum_scatter(partial, "tensor", scatter_dimension=0, tiled=True)[0]
 
+    asked, _ = lax.optimization_barrier((asked, partial))
     picked_a = local_call(
         pick_kernel, shaped((replicas,) + store_a.shape[1:], bf16), 0, 4 << 20,
         [SMEM, VMEM], HBM, [DMA((replicas,))], (asked, store_a), limit=ALL,
@@ -159,23 +180,28 @@
         [SMEM, SMEM, SMEM, SMEM, VMEM], (HBM, VMEM), [DMA((replicas,))],
         (asked, adapter_lists, placement_map, request_slot, store_b),
     )
+    me = lax.axis_index("tensor").astype(i32).reshape(1)
+    half = shaped((rows // 2, rank), f32)
+    mine, other = local_call(
+        shrink_kernel, (half, half), LONG, 3 << 20,
+        [SMEM] + [VMEM] * 3, (VMEM, VMEM), [pltpu.VMEM((rows, rank), f32)], (me, hold, x, got_a),
+    )
+    picked_b, other = lax.optimization_barrier((picked_b, other))
     got_b = lax.all_to_all(picked_b, "dp", split_axis=0, concat_axis=0, tiled=True)
 
-    shrink = local_call(
-        shrink_kernel, shaped((rows, rank), f32), 2 * rows * replicas * depth * rank, 3 << 20,
-        [VMEM] * 3, VMEM, [], (hold, x, got_a),
-    )
+    mine = local_call(add_kernel, half, ADD_LONG, 1 << 17, [VMEM, VMEM], VMEM, [],
+                      (mine, across(other, 1, columns)))
     bit = columns // 2
     while bit > 1:
-        shrink = shrink + across(shrink, bit, columns)
+        mine = mine + across(mine, bit, columns)
         bit //= 2
     out = local_call(
-        final_kernel, shaped((rows, width), bf16),
-        4 * rows * replicas * rank * width, 3 << 20,
-        [VMEM, VMEM, VMEM, HBM, HBM], VMEM,
-        [pltpu.VMEM((rows, width), f32), pltpu.VMEM(got_b.shape, bf16),
-         pltpu.VMEM((rows, width), f32), DMA((min(MOST_CHUNKS, replicas) + 1,))],
-        (hold, shrink, across(shrink, 1, columns), got_b, base), limit=40,
+        final_kernel, shaped((rows, width), bf16), LONG, 3 << 20,
+        [SMEM, VMEM, VMEM, VMEM, HBM, HBM], VMEM,
+        [pltpu.VMEM((rows, rank), f32), pltpu.VMEM((rows, width), f32),
+         pltpu.VMEM(got_b.shape, bf16), pltpu.VMEM((rows, width), f32),
+         DMA((min(MOST_CHUNKS, replicas) + 1,))],
+        (me, hold, mine, across(mine, 1, columns), got_b, base), limit=40,
     )
     return out.reshape(steps, requests, width)
 

time: 136 us -> 129 us (0.949)
  blocking collectives: 14.7 us -> 0 us
  waiting for transfers between devices: 34.3 us -> 43.2 us
  Pallas kernels: 18.1 us -> 16.1 us
    all_to_all x1 -> x0, blocking collectives: 14.7 us -> none  [on_device(): asked = lax.all_to_all(wish, 'dp', split_axis=0, concat_axis=0, tiled=True)]
    all_to_all x0 -> x1, starting transfers between devices: none -> 9.37 us  [on_device(): asked = lax.all_to_all(wish, 'dp', split_axis=0, concat_axis=0, tiled=True)]
    ppermute x4 -> x5, starting transfers between devices: 35.9 us -> 28 us  [across(): return lax.ppermute(value, 'tensor', [(i, i ^ bit) for i in range(size)])]
    ppermute x4 -> x5, waiting for transfers between devices: 14.6 us -> 19.1 us  [across(): return lax.ppermute(value, 'tensor', [(i, i ^ bit) for i in range(size)])]
    all_to_all x1, waiting for transfers between devices: 19.7 us -> 23.1 us  [on_device(): lax.all_to_all(picked_a, 'dp', split_axis=0, concat_axis=0, tiled=True)]
    pallas_call x6 -> x7, Pallas kernels: 18.1 us -> 16.1 us  [local_call(): pl.pallas_call(body, out_shape=outs, grid=grid, in_specs=in_specs, out_sp...]
    unnamed x16 -> x20, local copies, waits for them, and re-layouts: 2.95 us -> 2.88 us
  transfers between devices with their start and end apart: 7 -> 9, of which waited for: 5 -> 6; matrix products, arithmetic and copies ran while one was open for 0% -> 0% of each run, Pallas kernels for 7% -> 9%
where the time goes in v3:
time: 129 us; the launch traced here: 128 us
  starting transfers between devices  52.3 us (41%)
  waiting for transfers between devices  43.2 us (33%)
  Pallas kernels  16.1 us (12%)
  between operations  13.6 us (11%)
  local copies, waits for them, and re-layouts  2.88 us (2%)
    ppermute x5, starting transfers between devices, across(): return lax.ppermute(value, 'tensor', [(i, i ^ bit) for i in range(size)])  28 us
    all_to_all x1, waiting for transfers between devices, on_device(): lax.all_to_all(picked_a, 'dp', split_axis=0, concat_axis=0, tiled=True)  23.1 us
    ppermute x5, waiting for transfers between devices, across(): return lax.ppermute(value, 'tensor', [(i, i ^ bit) for i in range(size)])  19.1 us
    pallas_call x7, Pallas kernels, local_call(): pl.pallas_call(body, out_shape=outs, grid=grid, in_specs=in_specs, out_sp...  16.1 us
    all_to_all x1, starting transfers between devices, on_device(): asked = lax.all_to_all(wish, 'dp', split_axis=0, concat_axis=0, tiled=True)  9.37 us
    all_to_all x1, starting transfers between devices, on_device(): lax.all_to_all(picked_b, 'dp', split_axis=0, concat_axis=0, tiled=True)  8.36 us
    all_to_all x1, starting transfers between devices, on_device(): lax.all_to_all(picked_a, 'dp', split_axis=0, concat_axis=0, tiled=True)  6.62 us
    unnamed x20, local copies, waits for them, and re-layouts  2.88 us
  transfers between devices with their start and end apart: 9, of which 6 were waited for; matrix products, arithmetic and copies ran while one was open for 0% of the time, Pallas kernels for 9%

profile of v3, /device:TPU:6, one launch (start us, length us, event | category | flops | bytes accessed | tf_op | source)
XLA Modules:
  0.0 128.2 jit_solution(4259506868724176737)
XLA Ops:
  6.5 0.0 copy-start.4
  6.5 0.7 copy-done.4
  7.2 0.0 copy-start.6
  7.2 0.7 copy-done.6
  7.8 1.2 shard_map.73
  9.0 9.4 %all-to-all-start = ((s32[32,1,128]{2,1,0:T(1,128)}), s32[32,1,128]{2,1,0:T(1,128)S(1)}, u32[]{:S(2)}, u32[]{:S(2)}) async-start(s32[32,1,128]{2,1,0:T(1,128)} %shard_map.73), calls=%async_computation | async-start | bytes 32768 | tf_op jit(solution)/shard_map/all_to_all | solution.py:159
  18.4 0.0 reduce-scatter.2.cloned.1.call-start
  18.5 4.5 %shard_map.74 = f32[16,192,256]{2,1,0:T(8,128)} custom-call(bf16[192,256]{1,0:T(8,128)(2,1)} %bitcast.4, bf16[256,4096]{1,0:T(8,128)(2,1)} %weight_ref.1), custom_call_target="tpu_custom_call" | custom-call | flops 402653184 | bytes 5242880 | tf_op jit(solution)/shard_map/pallas_call | solution.py:18
  22.9 0.0 reduce-scatter.2.cloned.1.call-update
  23.0 1.0 all-to-all-done.refs_0_.asked_ref
  24.0 0.0 copy-start.1
  24.0 0.6 copy-done.1
  24.6 2.6 %shard_map.76 = bf16[32,256,128]{2,1,0:T(8,128)(2,1)} custom-call(s32[32,1,128]{2,1,0:T(1,128)} %copy-done.1, bf16[4,256,128]{2,1,0:T(8,128)(2,1)} %store_ref.1), custom_call_target="tpu_custom_call" | custom-call | bytes 4194304 | tf_op jit(solution)/shard_map/pallas_call | solution.py:18
  27.2 0.0 copy-start
  27.2 0.0 copy-start.2
  27.2 0.0 copy-start.5
  27.2 0.0 copy-start.7
  27.2 0.0 copy-start.8
  27.2 0.0 copy-start.3
  27.2 6.6 %all-to-all-start.1 = ((bf16[32,256,128]{2,1,0:T(8,128)(2,1)}), bf16[32,256,128]{2,1,0:T(8,128)(2,1)S(1)}, u32[]{:S(2)}, u32[]{:S(2)}) async-start(bf16[32,256,128]{2,1,0:T(8,128)(2,1)} %shard_map.76), calls=%async_computation.1 | async-start | bytes 4194304 | tf_op jit(solution)/shard_map/all_to_all | solution.py:176
  33.9 0.0 copy-done
  33.9 0.0 copy-done.2
  33.9 0.0 copy-done.5
  33.9 0.0 copy-done.7
  33.9 0.0 copy-done.8
  33.9 2.5 %shard_map.75 = (bf16[32,128,256]{2,1,0:T(8,128)(2,1)}, s32[192,128]{1,0:T(8,128)S(1)}) custom-call(s32[32,1,128]{2,1,0:T(1,128)S(1)} %copy-done.2, s32[1,16]{1,0:T(1,128)S(1)} %copy-done.5, s32[128]{0:T(128)S(1)} %copy-done.7, s32[64]{0:T(128)S(1)} %copy-done.8, bf16[4,128,256]{2,1,0:T(8,128)(2,1)S(1)} %copy-done), custom_call_target="tpu_custom_call" | custom-call | bytes 4194304 | tf_op jit(solution)/shard_map/pallas_call | solution.py:18
  36.4 23.1 %all-to-all-done.1.panels_ref = bf16[32,256,128]{2,1,0:T(8,128)(2,1)S(1)} async-done(((bf16[32,256,128]{2,1,0:T(8,128)(2,1)}), bf16[32,256,128]{2,1,0:T(8,128)(2,1)S(1)}, u32[]{:S(2)}, u32[]{:S(2)}) %all-to-all-start.1) | async-done | bytes 2097184 | tf_op jit(solution)/shard_map/all_to_all | solution.py:176
  59.4 0.0 copy-done.3
  59.5 2.1 %shard_map.77 = (f32[96,128]{1,0:T(8,128)S(1)}, f32[96,128]{1,0:T(8,128)S(1)}) custom-call(s32[1]{0:T(128)} %bitcast.me_ref, s32[192,128]{1,0:T(8,128)S(1)} %get-tuple-element.13.hold_ref, bf16[192,256]{1,0:T(8,128)(2,1)S(1)} %bitcast.5, bf16[32,256,128]{2,1,0:T(8,128)(2,1)S(1)} %all-to-all-done.1.panels_ref), custom_call_target="tpu_custom_call" | custom-call | flops 22749999104 | bytes 3145728 | tf_op jit(solution)/shard_map/pallas_call | solution.py:18
  61.5 1.9 %collective-permute-start = (f32[96,128]{1,0:T(8,128)S(1)}, f32[96,128]{1,0:T(8,128)S(1)}, u32[]{:S(2)}, u32[]{:S(2)}) collective-permute-start(f32[96,128]{1,0:T(8,128)S(1)} %get-tuple-element.17), channel_id=1, source_target_pairs={{0,1},{1,0},{2,3},{3,2},{4,5},{5,4},{6,7},{7,6},{8,9},{9,8},{10,11... | collective-permute-start | bytes 147464 | tf_op jit(solution)/shard_map/ppermute | solution.py:141
  63.5 8.4 %all-to-all-start.2 = ((bf16[32,128,256]{2,1,0:T(8,128)(2,1)}), bf16[32,128,256]{2,1,0:T(8,128)(2,1)S(1)}, u32[]{:S(2)}, u32[]{:S(2)}) async-start(bf16[32,128,256]{2,1,0:T(8,128)(2,1)} %get-tuple-element.18), calls=%async_computation.2 | async-start | bytes 4194304 | tf_op jit(solution)/shard_map/all_to_all | solution.py:190
  71.9 0.0 collective-permute-done.b_ref
  71.9 14.8 %collective-permute-start.1 = (f32[96,128]{1,0:T(8,128)S(1)}, f32[96,128]{1,0:T(8,128)S(1)}, u32[]{:S(2)}, u32[]{:S(2)}) collective-permute-start(f32[96,128]{1,0:T(8,128)S(1)} %shard_map.78), channel_id=1, source_target_pairs={{0,8},{1,9},{2,10},{3,11},{4,12},{5,13},{6,14},{7,15},{8,0},{9,1},... | collective-permute-start | bytes 147464 | tf_op jit(solution)/shard_map/ppermute | solution.py:141
  86.7 4.6 %collective-permute-done.1 = f32[96,128]{1,0:T(8,128)S(1)} collective-permute-done((f32[96,128]{1,0:T(8,128)S(1)}, f32[96,128]{1,0:T(8,128)S(1)}, u32[]{:S(2)}, u32[]{:S(2)}) %collective-permute-start.1) | collective-permute-done | bytes 49184 | tf_op jit(solution)/shard_map/ppermute | solution.py:141
  91.3 7.1 %collective-permute-start.2 = (f32[96,128]{1,0:T(8,128)S(1)}, f32[96,128]{1,0:T(8,128)S(1)}, u32[]{:S(2)}, u32[]{:S(2)}) collective-permute-start(f32[96,128]{1,0:T(8,128)S(1)} %add.11), channel_id=1, source_target_pairs={{0,4},{1,5},{2,6},{3,7},{4,0},{5,1},{6,2},{7,3},{8,12},{9,13},{10,... | collective-permute-start | bytes 147464 | tf_op jit(solution)/shard_map/ppermute | solution.py:141
  98.4 5.7 %collective-permute-done.2 = f32[96,128]{1,0:T(8,128)S(1)} collective-permute-done((f32[96,128]{1,0:T(8,128)S(1)}, f32[96,128]{1,0:T(8,128)S(1)}, u32[]{:S(2)}, u32[]{:S(2)}) %collective-permute-start.2) | collective-permute-done | bytes 49184 | tf_op jit(solution)/shard_map/ppermute | solution.py:141
  104.2 2.2 %collective-permute-start.3 = (f32[96,128]{1,0:T(8,128)S(1)}, f32[96,128]{1,0:T(8,128)S(1)}, u32[]{:S(2)}, u32[]{:S(2)}) collective-permute-start(f32[96,128]{1,0:T(8,128)S(1)} %add.12), channel_id=1, source_target_pairs={{0,2},{1,3},{2,0},{3,1},{4,6},{5,7},{6,4},{7,5},{8,10},{9,11},{10,... | collective-permute-start | bytes 147464 | tf_op jit(solution)/shard_map/ppermute | solution.py:141
  106.4 4.7 %collective-permute-done.3 = f32[96,128]{1,0:T(8,128)S(1)} collective-permute-done((f32[96,128]{1,0:T(8,128)S(1)}, f32[96,128]{1,0:T(8,128)S(1)}, u32[]{:S(2)}, u32[]{:S(2)}) %collective-permute-start.3) | collective-permute-done | bytes 49184 | tf_op jit(solution)/shard_map/ppermute | solution.py:141
  111.1 1.9 %collective-permute-start.4 = (f32[96,128]{1,0:T(8,128)S(1)}, f32[96,128]{1,0:T(8,128)S(1)}, u32[]{:S(2)}, u32[]{:S(2)}) collective-permute-start(f32[96,128]{1,0:T(8,128)S(1)} %add.13.mine_ref), channel_id=1, source_target_pairs={{0,1},{1,0},{2,3},{3,2},{4,5},{5,4},{6,7},{7,6},{8,9},{9,8},{10,11... | collective-permute-start | bytes 147464 | tf_op jit(solution)/shard_map/ppermute | solution.py:141
  113.0 4.1 %collective-permute-done.4.other_ref = f32[96,128]{1,0:T(8,128)S(1)} collective-permute-done((f32[96,128]{1,0:T(8,128)S(1)}, f32[96,128]{1,0:T(8,128)S(1)}, u32[]{:S(2)}, u32[]{:S(2)}) %collective-permute-start.4) | collective-permute-done | bytes 49184 | tf_op jit(solution)/shard_map/ppermute | solution.py:141
  117.0 0.0 all-to-all-done.2.panels_hbm
  117.0 0.0 reduce-scatter.2.cloned.1.call-done
  117.0 0.0 copy-start.9
  117.0 0.9 copy-done.9
  118.0 3.3 %shard_map.79 = bf16[192,256]{1,0:T(8,128)(2,1)} custom-call(s32[1]{0:T(128)} %bitcast.me_ref, s32[192,128]{1,0:T(8,128)S(1)} %get-tuple-element.13.hold_ref, f32[96,128]{1,0:T(8,128)S(1)} %add.13.mine_ref, f32[96,128]{1,0:T(8,128)S(1)} %collective-permute-done.4.other_ref, bf16[32,128,256]{2,1,0:T(8,128)(2,1)S(1)} %all-to-all-done.2.panels_hbm, ...), custom_call_target="tpu_custom_call" | custom-call | flops 22749999104 | bytes 3145728 | tf_op jit(solution)/shard_map/pallas_call | solution.py:18
  (4 shorter events, 0.0 us)
Async XLA Ops:
  6.5 0.7 copy-start.4
  7.2 0.7 copy-start.6
  9.0 14.9 %all-to-all-start = ((s32[32,1,128]{2,1,0:T(1,128)}), s32[32,1,128]{2,1,0:T(1,128)S(1)}, u32[]{:S(2)}, u32[]{:S(2)}) async-start(s32[32,1,128]{2,1,0:T(1,128)} %shard_map.73), calls=%async_computation | async-start | bytes 32768 | tf_op jit(solution)/shard_map/all_to_all | solution.py:159
  18.4 98.6 %reduce-scatter.2.cloned.1.call-start = ((), (), s32[]{:S(2)}) async-start(), calls=%async_computation.4 | async-start | bytes 3342336 | tf_op jit(solution)/shard_map/reduce_scatter | solution.py:169
  24.0 0.6 copy-start.1
  27.2 6.7 %copy-start = (bf16[4,128,256]{2,1,0:T(8,128)(2,1)S(1)}, bf16[4,128,256]{2,1,0:T(8,128)(2,1)}, u32[]{:S(2)}) copy-start(bf16[4,128,256]{2,1,0:T(8,128)(2,1)} %refs_4_.1) | copy-start | bytes 786436
  27.2 6.7 %copy-start.2 = (s32[32,1,128]{2,1,0:T(1,128)S(1)}, s32[32,1,128]{2,1,0:T(1,128)}, u32[]{:S(2)}) copy-start(s32[32,1,128]{2,1,0:T(1,128)} %copy-done.1) | copy-start | bytes 49156
  27.2 6.7 %copy-start.5 = (s32[1,16]{1,0:T(1,128)S(1)}, s32[1,16]{1,0:T(1,128)}, u32[]{:S(2)}) copy-start(s32[1,16]{1,0:T(1,128)} %refs_1_.3) | copy-start | bytes 196
  27.2 6.7 %copy-start.7 = (s32[128]{0:T(128)S(1)}, s32[128]{0:T(128)}, u32[]{:S(2)}) copy-start(s32[128]{0:T(128)} %refs_2_.1) | copy-start | bytes 1540
  27.2 6.7 %copy-start.8 = (s32[64]{0:T(128)S(1)}, s32[64]{0:T(128)}, u32[]{:S(2)}) copy-start(s32[64]{0:T(128)} %refs_3_.1) | copy-start | bytes 772
  27.2 32.2 %copy-start.3 = (bf16[3,64,256]{2,1,0:T(8,128)(2,1)S(1)}, bf16[3,64,256]{2,1,0:T(8,128)(2,1)}, u32[]{:S(2)}) copy-start(bf16[3,64,256]{2,1,0:T(8,128)(2,1)} %param.7) | copy-start | bytes 294916
  27.2 32.2 %all-to-all-start.1 = ((bf16[32,256,128]{2,1,0:T(8,128)(2,1)}), bf16[32,256,128]{2,1,0:T(8,128)(2,1)S(1)}, u32[]{:S(2)}, u32[]{:S(2)}) async-start(bf16[32,256,128]{2,1,0:T(8,128)(2,1)} %shard_map.76), calls=%async_computation.1 | async-start | bytes 4194304 | tf_op jit(solution)/shard_map/all_to_all | solution.py:176
  61.5 10.3 %collective-permute-start = (f32[96,128]{1,0:T(8,128)S(1)}, f32[96,128]{1,0:T(8,128)S(1)}, u32[]{:S(2)}, u32[]{:S(2)}) collective-permute-start(f32[96,128]{1,0:T(8,128)S(1)} %get-tuple-element.17), channel_id=1, source_target_pairs={{0,1},{1,0},{2,3},{3,2},{4,5},{5,4},{6,7},{7,6},{8,9},{9,8},{10,11... | collective-permute-start | bytes 147464 | tf_op jit(solution)/shard_map/ppermute | solution.py:141
  63.5 53.6 %all-to-all-start.2 = ((bf16[32,128,256]{2,1,0:T(8,128)(2,1)}), bf16[32,128,256]{2,1,0:T(8,128)(2,1)S(1)}, u32[]{:S(2)}, u32[]{:S(2)}) async-start(bf16[32,128,256]{2,1,0:T(8,128)(2,1)} %get-tuple-element.18), calls=%async_computation.2 | async-start | bytes 4194304 | tf_op jit(solution)/shard_map/all_to_all | solution.py:190
  71.9 19.5 %collective-permute-start.1 = (f32[96,128]{1,0:T(8,128)S(1)}, f32[96,128]{1,0:T(8,128)S(1)}, u32[]{:S(2)}, u32[]{:S(2)}) collective-permute-start(f32[96,128]{1,0:T(8,128)S(1)} %shard_map.78), channel_id=1, source_target_pairs={{0,8},{1,9},{2,10},{3,11},{4,12},{5,13},{6,14},{7,15},{8,0},{9,1},... | collective-permute-start | bytes 147464 | tf_op jit(solution)/shard_map/ppermute | solution.py:141
  91.3 12.8 %collective-permute-start.2 = (f32[96,128]{1,0:T(8,128)S(1)}, f32[96,128]{1,0:T(8,128)S(1)}, u32[]{:S(2)}, u32[]{:S(2)}) collective-permute-start(f32[96,128]{1,0:T(8,128)S(1)} %add.11), channel_id=1, source_target_pairs={{0,4},{1,5},{2,6},{3,7},{4,0},{5,1},{6,2},{7,3},{8,12},{9,13},{10,... | collective-permute-start | bytes 147464 | tf_op jit(solution)/shard_map/ppermute | solution.py:141
  104.2 6.9 %collective-permute-start.3 = (f32[96,128]{1,0:T(8,128)S(1)}, f32[96,128]{1,0:T(8,128)S(1)}, u32[]{:S(2)}, u32[]{:S(2)}) collective-permute-start(f32[96,128]{1,0:T(8,128)S(1)} %add.12), channel_id=1, source_target_pairs={{0,2},{1,3},{2,0},{3,1},{4,6},{5,7},{6,4},{7,5},{8,10},{9,11},{10,... | collective-permute-start | bytes 147464 | tf_op jit(solution)/shard_map/ppermute | solution.py:141
  111.1 6.0 %collective-permute-start.4 = (f32[96,128]{1,0:T(8,128)S(1)}, f32[96,128]{1,0:T(8,128)S(1)}, u32[]{:S(2)}, u32[]{:S(2)}) collective-permute-start(f32[96,128]{1,0:T(8,128)S(1)} %add.13.mine_ref), channel_id=1, source_target_pairs={{0,1},{1,0},{2,3},{3,2},{4,5},{5,4},{6,7},{7,6},{8,9},{9,8},{10,11... | collective-permute-start | bytes 147464 | tf_op jit(solution)/shard_map/ppermute | solution.py:141
  117.0 0.9 copy-start.9
Sparse Core Ops, SparseCore 0:
  23.1 84.1 reduce-scatter.1

commit v4 on v2

v4 whole, which is shorter than its diff:
```python
import jax
import jax.numpy as jnp
from jax import lax
from jax.experimental import pallas as pl
from jax.experimental.pallas import tpu as pltpu
from jax.sharding import PartitionSpec as P

MIB = 1024 * 1024
SMEM, VMEM, HBM = (pl.BlockSpec(memory_space=m) for m in (pltpu.SMEM, pltpu.VMEM, pltpu.HBM))
DMA = pltpu.SemaphoreType.DMA
MOST_PARTS = 8
ALL = 60


def local_call(body, outs, flops, moved, in_specs, out_specs, scratch, operands, grid=(), limit=16):
    return pl.pallas_call(
        body,
        out_shape=outs,
        grid=grid,
        in_specs=in_specs,
        out_specs=out_specs,
        scratch_shapes=scratch,
        compiler_params=pltpu.CompilerParams(vmem_limit_bytes=limit * MIB),
        cost_estimate=pl.CostEstimate(flops=flops, bytes_accessed=moved, transcendentals=0),
    )(*operands)


def wish_kernel(stored, list_ref, place_ref, wish_ref):
    wish_ref[...] = jnp.zeros_like(wish_ref)
    for s in range(list_ref.shape[1]):
        position = place_ref[list_ref[0, s]]
        slot = lax.rem(position, stored)
        wish_ref[lax.div(position, stored)] = jnp.full(wish_ref.shape[1:], slot, jnp.int32)


def base_kernel(x_ref, weight_ref, out_ref):
    x = x_ref[...]
    width = out_ref.shape[2]
    for c in range(out_ref.shape[0]):
        out_ref[c] = jnp.dot(
            x, weight_ref[:, c * width:(c + 1) * width], preferred_element_type=jnp.float32
        )


def pick_kernel(stored, steps, asked_ref, list_ref, place_ref, slot_ref, a_ref, b_ref,
                out_ref, hold_ref, sems):
    count = out_ref.shape[0]
    depth, width = a_ref.shape[1], b_ref.shape[2]
    rank = b_ref.shape[1]

    def copies(q):
        n = asked_ref[q, 0, 0]
        yield pltpu.make_async_copy(a_ref.at[n], out_ref.at[q, pl.ds(0, depth)], sems.at[q, 0])
        for c in range(width // 128):
            yield pltpu.make_async_copy(
                b_ref.at[n, :, pl.ds(c * 128, 128)],
                out_ref.at[q, pl.ds(depth + c * rank, rank)], sems.at[q, c + 1],
            )

    @pl.loop(0, count)
    def _(q):
        for copy in copies(q):
            copy.start()

    requests = slot_ref.shape[0]

    @pl.loop(0, requests, unroll=8)
    def _(r):
        holder = lax.div(place_ref[list_ref[0, slot_ref[r]]], stored)
        for step in range(steps):
            hold_ref[pl.ds(step * requests + r, 1), :] = jnp.full((1, 128), holder, jnp.int32)

    @pl.loop(0, count)
    def _(q):
        for copy in copies(q):
            copy.wait()


def by_parts(copies):
    for part in copies:
        for copy in part:
            copy.start()
    return lambda c: [copy.wait() for copy in copies[c]]


def shrink_kernel(hold_ref, x_ref, panels_hbm, out_ref, total_ref, panels_ref, sems):
    each = panels_ref.shape[0] // sems.shape[0]
    depth = panels_ref.shape[1]
    ready = by_parts([
        [pltpu.make_async_copy(panels_hbm.at[pl.ds(c * each, each), pl.ds(0, depth)],
                               panels_ref.at[pl.ds(c * each, each)], sems.at[c])]
        for c in range(sems.shape[0])
    ])
    hold = hold_ref[...]
    x = x_ref[...]
    total_ref[...] = jnp.zeros_like(total_ref)
    for c in range(sems.shape[0]):
        ready(c)
        for q in range(c * each, (c + 1) * each):
            product = jnp.dot(x, panels_ref[q], preferred_element_type=jnp.float32)
            total_ref[...] = jnp.where(hold == q, product, total_ref[...])

    share = out_ref.shape[1]
    for z in range(out_ref.shape[0]):
        if z * share < total_ref.shape[0]:
            out_ref[z] = total_ref[z * share:(z + 1) * share, :]
        else:
            out_ref[z] = jnp.zeros(out_ref.shape[1:], jnp.float32)


def final_kernel(hold_ref, shrink_ref, panels_hbm, base_ref, out_ref, total_ref, panels_ref, sems):
    rows, width = out_ref.shape
    rank = shrink_ref.shape[2]
    depth = panels_hbm.shape[1] - rank * (width // 128)
    each = panels_ref.shape[0] // sems.shape[0]
    ready = by_parts([
        [pltpu.make_async_copy(
            panels_hbm.at[pl.ds(c * each, each), pl.ds(depth + k * rank, rank)],
            panels_ref.at[pl.ds(c * each, each), :, pl.ds(k * 128, 128)], sems.at[c, k])
         for k in range(width // 128)]
        for c in range(sems.shape[0])
    ])
    hold = hold_ref[...]
    hold = jnp.concatenate([hold] * (width // 128), axis=1)
    share = shrink_ref.shape[1]
    shrink = jnp.concatenate([shrink_ref[z] for z in range(rows // share)], axis=0)
    high = shrink.astype(jnp.bfloat16)
    low = (shrink - high.astype(jnp.float32)).astype(jnp.bfloat16)
    both = jnp.concatenate([high, low], axis=1)
    total_ref[...] = jnp.zeros_like(total_ref)
    for c in range(sems.shape[0]):
        ready(c)
        for q in range(c * each, (c + 1) * each):
            panel = panels_ref[q]
            product = jnp.dot(
                both, jnp.concatenate([panel, panel], axis=0), preferred_element_type=jnp.float32
            )
            total_ref[...] = jnp.where(hold == q, product, total_ref[...])

    out_ref[...] = (base_ref[...] + total_ref[...]).astype(out_ref.dtype)


def on_device(attn_out, base_weight, store_a, store_b, adapter_lists, placement_map, request_slot):
    replicas = lax.axis_size("dp")
    columns = lax.axis_size("tensor")
    stored, depth, rank = store_a.shape
    steps, requests, _ = attn_out.shape
    width = store_b.shape[2]
    rows = steps * requests
    f32, bf16, i32 = jnp.float32, jnp.bfloat16, jnp.int32
    shaped = jax.ShapeDtypeStruct
    x = attn_out.reshape(rows, depth)

    wish = local_call(
        lambda *refs: wish_kernel(stored, *refs), shaped((replicas, 1, 128), i32), 0, 1 << 14,
        [SMEM, SMEM], VMEM, [], (adapter_lists, placement_map), limit=ALL,
    )
    asked = lax.all_to_all(wish, "dp", split_axis=0, concat_axis=0, tiled=True)

    partial = local_call(
        base_kernel, shaped((columns, rows, width), f32),
        2 * rows * depth * columns * width, 5 << 20,
        [pl.BlockSpec((rows, depth), lambda i: (0, 0)),
         pl.BlockSpec((depth, 4 * width), lambda i: (0, i))],
        pl.BlockSpec((4, rows, width), lambda i: (i, 0, 0)), [], (x, base_weight),
        grid=(columns // 4,), limit=ALL,
    )
    base = lax.psum_scatter(partial, "tensor", scatter_dimension=0, tiled=True)[0]

    picked, hold = local_call(
        lambda *refs: pick_kernel(stored, steps, *refs),
        (shaped((replicas, depth + rank * (width // 128), 128), bf16), shaped((rows, 128), i32)),
        0, 8 << 20, [SMEM] * 4 + [VMEM] * 2, (HBM, VMEM), [DMA((replicas, 1 + width // 128))],
        (asked, adapter_lists, placement_map, request_slot, store_a, store_b), limit=ALL,
    )
    panels = lax.all_to_all(picked, "dp", split_axis=0, concat_axis=0, tiled=True)

    share = 16
    parts = min(MOST_PARTS, replicas)
    part = local_call(
        shrink_kernel, shaped((columns, share, rank), f32), 2 * rows * replicas * depth * rank,
        3 << 20, [VMEM, VMEM, HBM], VMEM,
        [pltpu.VMEM((rows, rank), f32), pltpu.VMEM((replicas, depth, rank), bf16), DMA((parts,))],
        (hold, x, panels), limit=ALL,
    )
    part = lax.all_to_all(part, "tensor", split_axis=0, concat_axis=0, tiled=True)
    mine = jnp.broadcast_to(jnp.sum(part, axis=0)[None], part.shape)
    shrink = lax.all_to_all(mine, "tensor", split_axis=0, concat_axis=0, tiled=True)
    out = local_call(
        final_kernel, shaped((rows, width), bf16), 4 * rows * replicas * rank * width, 3 << 20,
        [VMEM, VMEM, HBM, VMEM], VMEM,
        [pltpu.VMEM((rows, width), f32), pltpu.VMEM((replicas, rank, width), bf16),
         DMA((parts, width // 128))],
        (hold, shrink, panels, base), limit=ALL,
    )
    return out.reshape(steps, requests, width)


def solution(mesh):
    placed = (
        P(None, "dp", "tensor"),
        P("tensor", None),
        P("dp", "tensor", None),
        P("dp", None, "tensor"),
        P("dp", None),
        P(),
        P("dp"),
    )
    return jax.shard_map(
        on_device, mesh=mesh, in_specs=placed, out_specs=P(None, "dp", "tensor"), check_vma=False
    )
```

time: 136 us -> 153 us (1.12)
  blocking collectives: 14.7 us -> 118 us
  starting transfers between devices: 51 us -> 0.01 us
  waiting for transfers between devices: 34.3 us -> 0.02 us
  local copies, waits for them, and re-layouts: 2.95 us -> 0.01 us
  Pallas kernels: 18.1 us -> 19.9 us
    all_to_all x0 -> x3, blocking collectives: none -> 102 us  [the longest x1 55 us: on_device(): lax.all_to_all(picked, 'dp', split_axis=0, concat_axis=0, tiled=True)]
    ppermute x4 -> x0, starting transfers between devices: 35.9 us -> none  [across(): return lax.ppermute(value, 'tensor', [(i, i ^ bit) for i in range(size)])]
    all_to_all x2 -> x0, waiting for transfers between devices: 19.7 us -> none  [the longest x1 19.7 us: on_device(): lax.all_to_all(picked_a, 'dp', split_axis=0, concat_axis=0, tiled=True)]
    all_to_all x2 -> x0, starting transfers between devices: 15.1 us -> none  [the longest x1 9.18 us: on_device(): lax.all_to_all(picked_b, 'dp', split_axis=0, concat_axis=0, tiled=True)]
    ppermute x4 -> x0, waiting for transfers between devices: 14.6 us -> none  [across(): return lax.ppermute(value, 'tensor', [(i, i ^ bit) for i in range(size)])]
    unnamed x16 -> x0, local copies, waits for them, and re-layouts: 2.95 us -> none
    pallas_call x6 -> x5, Pallas kernels: 18.1 us -> 19.9 us  [local_call(): pl.pallas_call(body, out_shape=outs, grid=grid, in_specs=in_specs, out_sp...]
  transfers between devices with their start and end apart: 7 -> 1, of which waited for: 5 -> 0; matrix products, arithmetic and copies ran while one was open for 0% -> 0% of each run, Pallas kernels for 7% -> 7%
where the time goes in v4:
time: 153 us; the launch traced here: 151 us
  blocking collectives  118 us (77%)
  Pallas kernels  19.9 us (13%)
  between operations  13.4 us (9%)
    all_to_all x1, blocking collectives, on_device(): lax.all_to_all(picked, 'dp', split_axis=0, concat_axis=0, tiled=True)  55 us
    all_to_all x1, blocking collectives, on_device(): lax.all_to_all(part, 'tensor', split_axis=0, concat_axis=0, tiled=True)  26.6 us
    all_to_all x1, blocking collectives, on_device(): lax.all_to_all(mine, 'tensor', split_axis=0, concat_axis=0, tiled=True)  20.7 us
    pallas_call x5, Pallas kernels, local_call(): pl.pallas_call(body, out_shape=outs, grid=grid, in_specs=in_specs, out_sp...  19.9 us
    all_to_all x1, blocking collectives, on_device(): asked = lax.all_to_all(wish, 'dp', split_axis=0, concat_axis=0, tiled=True)  15.4 us
  transfers between devices with their start and end apart: 1, of which 0 were waited for; matrix products, arithmetic and copies ran while one was open for 0% of the time, Pallas kernels for 7%

profile of v4, /device:TPU:6, one launch (start us, length us, event | category | flops | bytes accessed | tf_op | source)
XLA Modules:
  0.0 151.1 jit_solution(11062416236912582859)
XLA Ops:
  6.5 0.0 reduce-scatter.2.cloned.1.call-start
  6.5 4.5 %shard_map.76 = f32[16,192,256]{2,1,0:T(8,128)} custom-call(bf16[192,256]{1,0:T(8,128)(2,1)} %bitcast.3, bf16[256,4096]{1,0:T(8,128)(2,1)} %weight_ref.1), custom_call_target="tpu_custom_call" | custom-call | flops 402653184 | bytes 5242880 | tf_op jit(solution)/shard_map/pallas_call | solution.py:16
  11.0 0.0 reduce-scatter.2.cloned.1.call-update
  11.1 1.3 shard_map.73
  12.4 15.4 %all_to_all.20.refs_0_ = s32[32,1,128]{2,1,0:T(1,128)} all-to-all(s32[32,1,128]{2,1,0:T(1,128)} %shard_map.73), channel_id=1, replica_groups=mesh['dp'=32,'tensor'=16] {'dp'}, dimensions={0} | all-to-all | bytes 32768 | tf_op jit(solution)/shard_map/all_to_all | solution.py:158
  27.8 4.5 %shard_map.74 = (bf16[32,512,128]{2,1,0:T(8,128)(2,1)}, s32[192,128]{1,0:T(8,128)}) custom-call(s32[32,1,128]{2,1,0:T(1,128)} %all_to_all.20.refs_0_, s32[1,16]{1,0:T(1,128)} %refs_1_.3, s32[128]{0:T(128)} %refs_2_.1, s32[64]{0:T(128)} %refs_3_.1, bf16[4,256,128]{2,1,0:T(8,128)(2,1)} %refs_4_.1, bf16[4,128,256]{2,1,0:T(8,128)(2,1)} %refs_5_.1), custom_call_target="tpu_custom_call" | custom-call | bytes 8388608 | tf_op jit(solution)/shard_map/pallas_call | solution.py:16
  32.3 55.0 %all_to_all.21.panels_hbm = bf16[32,512,128]{2,1,0:T(8,128)(2,1)} all-to-all(bf16[32,512,128]{2,1,0:T(8,128)(2,1)} %get-tuple-element.8), channel_id=1, replica_groups=mesh['dp'=32,'tensor'=16] {'dp'}, dimensions={0} | all-to-all | bytes 8388608 | tf_op jit(solution)/shard_map/all_to_all | solution.py:176
  87.3 4.6 %shard_map.75 = f32[16,16,128]{2,1,0:T(8,128)} custom-call(s32[192,128]{1,0:T(8,128)} %get-tuple-element.7.hold_ref, bf16[192,256]{1,0:T(8,128)(2,1)} %bitcast.4, bf16[32,512,128]{2,1,0:T(8,128)(2,1)} %all_to_all.21.panels_hbm), custom_call_target="tpu_custom_call" | custom-call | flops 402653184 | bytes 3145728 | tf_op jit(solution)/shard_map/pallas_call | solution.py:16
  92.0 26.6 %all_to_all.22 = f32[16,16,128]{2,1,0:T(8,128)S(1)} all-to-all(f32[16,16,128]{2,1,0:T(8,128)} %shard_map.75), channel_id=1, replica_groups=mesh['dp'=32,'tensor'=16] {'tensor'}, dimensions={0} | all-to-all | bytes 262144 | tf_op jit(solution)/shard_map/all_to_all | solution.py:186
  118.6 20.7 %all_to_all.23.shrink_ref = f32[16,16,128]{2,1,0:T(8,128)} all-to-all(f32[16,16,128]{2,1,0:T(8,128)S(1)} %broadcast_in_dim.2), channel_id=1, replica_groups=mesh['dp'=32,'tensor'=16] {'tensor'}, dimensions={0} | all-to-all | bytes 262144 | tf_op jit(solution)/shard_map/all_to_all | solution.py:188
  139.3 0.0 reduce-scatter.2.cloned.1.call-done
  139.3 5.0 %shard_map.77 = bf16[192,256]{1,0:T(8,128)(2,1)} custom-call(s32[192,128]{1,0:T(8,128)} %get-tuple-element.7.hold_ref, f32[16,16,128]{2,1,0:T(8,128)} %all_to_all.23.shrink_ref, bf16[32,512,128]{2,1,0:T(8,128)(2,1)} %all_to_all.21.panels_hbm, f32[192,256]{1,0:T(8,128)} %bitcast.5), custom_call_target="tpu_custom_call" | custom-call | flops 805306368 | bytes 3145728 | tf_op jit(solution)/shard_map/pallas_call | solution.py:16
  (2 shorter events, 0.0 us)
Async XLA Ops:
  6.5 132.8 %reduce-scatter.2.cloned.1.call-start = ((), (), s32[]{:S(2)}) async-start(), calls=%async_computation.5 | async-start | bytes 3342336 | tf_op jit(solution)/shard_map/reduce_scatter | solution.py:168
Sparse Core Ops, SparseCore 0:
  11.2 80.6 reduce-scatter.1

commit v5 on v3

--- a/solution.py
+++ b/solution.py
@@ -8,8 +8,8 @@
 MIB = 1024 * 1024
 SMEM, VMEM, HBM = (pl.BlockSpec(memory_space=m) for m in (pltpu.SMEM, pltpu.VMEM, pltpu.HBM))
 DMA = pltpu.SemaphoreType.DMA
-MOST_CHUNKS = 8
-ADD_LONG = 2 * 10**10
+HALF_LONG = 10 ** 8
+ADD_LONG = 2*10**10
 LONG = 2275 * 10**7
 ALL = 60
 
@@ -99,42 +99,36 @@
             pl.ds(pl.multiple_of((1 - odd) * half, half), half))
 
 
-def final_kernel(me_ref, hold_ref, mine_ref, other_ref, panels_hbm, base_hbm, out_ref,
-                 shrink_ref, total_ref, panels_ref, base_ref, sems):
-    chunks = sems.shape[0] - 1
-    each = panels_ref.shape[0] // chunks
-
-    def copy(c):
-        part = pl.ds(c * each, each)
-        return pltpu.make_async_copy(panels_hbm.at[part], panels_ref.at[part], sems.at[c])
-
-    base_copy = pltpu.make_async_copy(base_hbm, base_ref, sems.at[chunks])
-    for c in range(chunks):
-        copy(c).start()
-    base_copy.start()
-
-    hold = hold_ref[...]
+def up(hold_ref, shrink_ref, rows, panels_ref, total_ref):
+    hold = hold_ref[rows, :]
     hold = jnp.concatenate([hold] * (total_ref.shape[1] // hold.shape[1]), axis=1)
-    mine, other = halves(me_ref, shrink_ref)
-    shrink_ref[mine, :] = mine_ref[...]
-    shrink_ref[other, :] = other_ref[...]
     shrink = shrink_ref[...]
     high = shrink.astype(jnp.bfloat16)
     low = (shrink - high.astype(jnp.float32)).astype(jnp.bfloat16)
     both = jnp.concatenate([high, low], axis=1)
     total_ref[...] = jnp.zeros_like(total_ref)
 
-    for c in range(chunks):
-        copy(c).wait()
-        for q in range(c * each, (c + 1) * each):
-            panel = panels_ref[q]
-            product = jnp.dot(
-                both, jnp.concatenate([panel, panel], axis=0), preferred_element_type=jnp.float32
-            )
-            total_ref[...] = jnp.where(hold == q, product, total_ref[...])
-
-    base_copy.wait()
-    out_ref[...] = (base_ref[...] + total_ref[...]).astype(out_ref.dtype)
+    @pl.loop(0, panels_ref.shape[0], unroll=4)
+    def _(q):
+        panel = panels_ref[q]
+        product = jnp.dot(
+            both, jnp.concatenate([panel, panel], axis=0), preferred_element_type=jnp.float32
+        )
+        total_ref[...] = jnp.where(hold == q, product, total_ref[...])
+
+
+def first_half_kernel(me_ref, hold_ref, shrink_ref, panels_ref, base_ref, out_ref, total_ref):
+    mine, other = halves(me_ref, base_ref)
+    up(hold_ref, shrink_ref, mine, panels_ref, total_ref)
+    out_ref[mine, :] = base_ref[mine, :] + total_ref[...]
+    out_ref[other, :] = base_ref[other, :]
+
+
+def second_half_kernel(me_ref, hold_ref, shrink_ref, panels_ref, sum_ref, out_ref, total_ref):
+    mine, other = halves(me_ref, sum_ref)
+    up(hold_ref, shrink_ref, other, panels_ref, total_ref)
+    out_ref[mine, :] = sum_ref[mine, :].astype(out_ref.dtype)
+    out_ref[other, :] = (sum_ref[other, :] + total_ref[...]).astype(out_ref.dtype)
 
 
 def across(value, bit, size):
@@ -154,7 +148,7 @@
 
     wish = local_call(
         lambda *refs: wish_kernel(stored, *refs), shaped((replicas, 1, 128), i32), 0, 1 << 14,
-        [SMEM, SMEM], VMEM, [], (adapter_lists, placement_map),
+        [SMEM, SMEM], VMEM, [], (adapter_lists, placement_map), limit=ALL,
     )
     asked = lax.all_to_all(wish, "dp", split_axis=0, concat_axis=0, tiled=True)
 
@@ -188,21 +182,20 @@
     )
     picked_b, other = lax.optimization_barrier((picked_b, other))
     got_b = lax.all_to_all(picked_b, "dp", split_axis=0, concat_axis=0, tiled=True)
-
     mine = local_call(add_kernel, half, ADD_LONG, 1 << 17, [VMEM, VMEM], VMEM, [],
                       (mine, across(other, 1, columns)))
-    bit = columns // 2
-    while bit > 1:
-        mine = mine + across(mine, bit, columns)
-        bit //= 2
-    out = local_call(
-        final_kernel, shaped((rows, width), bf16), LONG, 3 << 20,
-        [SMEM, VMEM, VMEM, VMEM, HBM, HBM], VMEM,
-        [pltpu.VMEM((rows, rank), f32), pltpu.VMEM((rows, width), f32),
-         pltpu.VMEM(got_b.shape, bf16), pltpu.VMEM((rows, width), f32),
-         DMA((min(MOST_CHUNKS, replicas) + 1,))],
-        (me, hold, mine, across(mine, 1, columns), got_b, base), limit=40,
-    )
+    mine = mine + across(mine, 2, columns)
+    mine = mine + across(mine, 4, columns)
+    mine = mine + across(mine, 8, columns)
+    other = across(mine, 1, columns)
+    def ends(kernel, cost, dtype, shrink, so_far):
+        return local_call(
+            kernel, shaped((rows, width), dtype), cost, 3 << 20, [SMEM] + [VMEM] * 4, VMEM,
+            [pltpu.VMEM((rows // 2, width), f32)], (me, hold, shrink, got_b, so_far),
+        )
+
+    out = ends(first_half_kernel, HALF_LONG, f32, mine, base)
+    out = ends(second_half_kernel, LONG, bf16, other, out)
     return out.reshape(steps, requests, width)
 
 

time: 129 us -> 125 us (0.969)
  waiting for transfers between devices: 43.2 us -> 34.5 us
  Pallas kernels: 16.1 us -> 19.3 us
  starting transfers between devices: 52.3 us -> 53.8 us
    ppermute x5, waiting for transfers between devices: 19.1 us -> 13.9 us  [across(): return lax.ppermute(value, 'tensor', [(i, i ^ bit) for i in range(size)])]
    all_to_all x1, waiting for transfers between devices: 23.1 us -> 19.6 us  [on_device(): lax.all_to_all(picked_a, 'dp', split_axis=0, concat_axis=0, tiled=True)]
    pallas_call x7 -> x8, Pallas kernels: 16.1 us -> 19.3 us  [local_call(): pl.pallas_call(body, out_shape=outs, grid=grid, in_specs=in_specs, out_sp...]
    ppermute x5, starting transfers between devices: 28 us -> 29.5 us  [across(): return lax.ppermute(value, 'tensor', [(i, i ^ bit) for i in range(size)])]
    unnamed x20 -> x18, local copies, waits for them, and re-layouts: 2.88 us -> 2.9 us
  transfers between devices with their start and end apart: 9 -> 9, of which waited for: 6 -> 6; matrix products, arithmetic and copies ran while one was open for 0% -> 0% of each run, Pallas kernels for 9% -> 12%
where the time goes in v5:
time: 125 us; the launch traced here: 124 us
  starting transfers between devices  53.8 us (43%)
  waiting for transfers between devices  34.5 us (28%)
  Pallas kernels  19.3 us (15%)
  between operations  13.6 us (11%)
  local copies, waits for them, and re-layouts  2.9 us (2%)
    ppermute x5, starting transfers between devices, across(): return lax.ppermute(value, 'tensor', [(i, i ^ bit) for i in range(size)])  29.5 us
    all_to_all x1, waiting for transfers between devices, on_device(): lax.all_to_all(picked_a, 'dp', split_axis=0, concat_axis=0, tiled=True)  19.6 us
    pallas_call x8, Pallas kernels, local_call(): pl.pallas_call(body, out_shape=outs, grid=grid, in_specs=in_specs, out_sp...  19.3 us
    ppermute x5, waiting for transfers between devices, across(): return lax.ppermute(value, 'tensor', [(i, i ^ bit) for i in range(size)])  13.9 us
    all_to_all x1, starting transfers between devices, on_device(): asked = lax.all_to_all(wish, 'dp', split_axis=0, concat_axis=0, tiled=True)  9.37 us
    all_to_all x1, starting transfers between devices, on_device(): lax.all_to_all(picked_b, 'dp', split_axis=0, concat_axis=0, tiled=True)  8.36 us
    all_to_all x1, starting transfers between devices, on_device(): lax.all_to_all(picked_a, 'dp', split_axis=0, concat_axis=0, tiled=True)  6.63 us
    unnamed x18, local copies, waits for them, and re-layouts  2.9 us
  transfers between devices with their start and end apart: 9, of which 6 were waited for; matrix products, arithmetic and copies ran while one was open for 0% of the time, Pallas kernels for 12%

profile of v5, /device:TPU:6, one launch (start us, length us, event | category | flops | bytes accessed | tf_op | source)
XLA Modules:
  0.0 124.3 jit_solution(6600766041179864772)
XLA Ops:
  6.5 1.3 %shard_map.73 = s32[32,1,128]{2,1,0:T(1,128)} custom-call(s32[1,16]{1,0:T(1,128)} %refs_1_.3, s32[128]{0:T(128)} %refs_2_.1), custom_call_target="tpu_custom_call" | custom-call | bytes 16384 | tf_op jit(solution)/shard_map/pallas_call | solution.py:18
  7.9 9.4 %all-to-all-start = ((s32[32,1,128]{2,1,0:T(1,128)}), s32[32,1,128]{2,1,0:T(1,128)S(1)}, u32[]{:S(2)}, u32[]{:S(2)}) async-start(s32[32,1,128]{2,1,0:T(1,128)} %shard_map.73), calls=%async_computation | async-start | bytes 32768 | tf_op jit(solution)/shard_map/all_to_all | solution.py:153
  17.2 0.0 reduce-scatter.2.cloned.1.call-start
  17.3 4.5 %shard_map.74 = f32[16,192,256]{2,1,0:T(8,128)} custom-call(bf16[192,256]{1,0:T(8,128)(2,1)} %bitcast.5, bf16[256,4096]{1,0:T(8,128)(2,1)} %weight_ref.1), custom_call_target="tpu_custom_call" | custom-call | flops 402653184 | bytes 5242880 | tf_op jit(solution)/shard_map/pallas_call | solution.py:18
  21.8 0.0 reduce-scatter.2.cloned.1.call-update
  21.8 1.0 all-to-all-done.refs_0_.asked_ref
  22.8 0.0 copy-start.3
  22.8 0.6 copy-done.3
  23.4 2.6 %shard_map.76 = bf16[32,256,128]{2,1,0:T(8,128)(2,1)} custom-call(s32[32,1,128]{2,1,0:T(1,128)} %copy-done.3, bf16[4,256,128]{2,1,0:T(8,128)(2,1)} %store_ref.1), custom_call_target="tpu_custom_call" | custom-call | bytes 4194304 | tf_op jit(solution)/shard_map/pallas_call | solution.py:18
  26.0 0.0 copy-start.1
  26.0 0.0 copy-start.4
  26.0 0.0 copy-start.6
  26.0 0.0 copy-start.7
  26.0 0.0 copy-start.8
  26.0 0.0 copy-start.5
  26.1 6.6 %all-to-all-start.1 = ((bf16[32,256,128]{2,1,0:T(8,128)(2,1)}), bf16[32,256,128]{2,1,0:T(8,128)(2,1)S(1)}, u32[]{:S(2)}, u32[]{:S(2)}) async-start(bf16[32,256,128]{2,1,0:T(8,128)(2,1)} %shard_map.76), calls=%async_computation.1 | async-start | bytes 4194304 | tf_op jit(solution)/shard_map/all_to_all | solution.py:170
  32.7 0.0 copy-done.1
  32.7 0.0 copy-done.4
  32.7 0.0 copy-done.6
  32.7 0.0 copy-done.7
  32.7 0.0 copy-done.8
  32.8 4.5 %shard_map.75 = (bf16[32,128,256]{2,1,0:T(8,128)(2,1)S(1)}, s32[192,128]{1,0:T(8,128)S(1)}) custom-call(s32[32,1,128]{2,1,0:T(1,128)S(1)} %copy-done.4, s32[1,16]{1,0:T(1,128)S(1)} %copy-done.6, s32[128]{0:T(128)S(1)} %copy-done.7, s32[64]{0:T(128)S(1)} %copy-done.8, bf16[4,128,256]{2,1,0:T(8,128)(2,1)S(1)} %copy-done.1), custom_call_target="tpu_custom_call" | custom-call | bytes 4194304 | tf_op jit(solution)/shard_map/pallas_call | solution.py:18
  37.3 0.0 copy-start
  37.3 1.3 %copy-done = bf16[32,128,256]{2,1,0:T(8,128)(2,1)} copy-done((bf16[32,128,256]{2,1,0:T(8,128)(2,1)}, bf16[32,128,256]{2,1,0:T(8,128)(2,1)S(1)}, u32[]{:S(2)}) %copy-start) | copy-done | bytes 2097176
  38.6 19.6 %all-to-all-done.1.panels_ref = bf16[32,256,128]{2,1,0:T(8,128)(2,1)S(1)} async-done(((bf16[32,256,128]{2,1,0:T(8,128)(2,1)}), bf16[32,256,128]{2,1,0:T(8,128)(2,1)S(1)}, u32[]{:S(2)}, u32[]{:S(2)}) %all-to-all-start.1) | async-done | bytes 2097184 | tf_op jit(solution)/shard_map/all_to_all | solution.py:170
  58.3 0.0 copy-done.5
  58.3 2.1 %shard_map.77 = (f32[96,128]{1,0:T(8,128)S(1)}, f32[96,128]{1,0:T(8,128)S(1)}) custom-call(s32[1]{0:T(128)} %bitcast.me_ref, s32[192,128]{1,0:T(8,128)S(1)} %get-tuple-element.13.hold_ref, bf16[192,256]{1,0:T(8,128)(2,1)S(1)} %bitcast.6, bf16[32,256,128]{2,1,0:T(8,128)(2,1)S(1)} %all-to-all-done.1.panels_ref), custom_call_target="tpu_custom_call" | custom-call | flops 22749999104 | bytes 3145728 | tf_op jit(solution)/shard_map/pallas_call | solution.py:18
  60.4 1.9 %collective-permute-start = (f32[96,128]{1,0:T(8,128)S(1)}, f32[96,128]{1,0:T(8,128)S(1)}, u32[]{:S(2)}, u32[]{:S(2)}) collective-permute-start(f32[96,128]{1,0:T(8,128)S(1)} %get-tuple-element.17), channel_id=1, source_target_pairs={{0,1},{1,0},{2,3},{3,2},{4,5},{5,4},{6,7},{7,6},{8,9},{9,8},{10,11... | collective-permute-start | bytes 147464 | tf_op jit(solution)/shard_map/ppermute | solution.py:135
  62.3 8.4 %all-to-all-start.2 = ((bf16[32,128,256]{2,1,0:T(8,128)(2,1)}), bf16[32,128,256]{2,1,0:T(8,128)(2,1)S(1)}, u32[]{:S(2)}, u32[]{:S(2)}) async-start(bf16[32,128,256]{2,1,0:T(8,128)(2,1)} %copy-done), calls=%async_computation.2 | async-start | bytes 4194304 | tf_op jit(solution)/shard_map/all_to_all | solution.py:184
  70.7 0.0 collective-permute-done.b_ref
  70.7 5.2 %collective-permute-start.1 = (f32[96,128]{1,0:T(8,128)S(1)}, f32[96,128]{1,0:T(8,128)S(1)}, u32[]{:S(2)}, u32[]{:S(2)}) collective-permute-start(f32[96,128]{1,0:T(8,128)S(1)} %shard_map.78), channel_id=1, source_target_pairs={{0,2},{1,3},{2,0},{3,1},{4,6},{5,7},{6,4},{7,5},{8,10},{9,11},{10,... | collective-permute-start | bytes 147464 | tf_op jit(solution)/shard_map/ppermute | solution.py:135
  75.9 4.4 %collective-permute-done.1 = f32[96,128]{1,0:T(8,128)S(1)} collective-permute-done((f32[96,128]{1,0:T(8,128)S(1)}, f32[96,128]{1,0:T(8,128)S(1)}, u32[]{:S(2)}, u32[]{:S(2)}) %collective-permute-start.1) | collective-permute-done | bytes 49184 | tf_op jit(solution)/shard_map/ppermute | solution.py:135
  80.2 8.5 %collective-permute-start.2 = (f32[96,128]{1,0:T(8,128)S(1)}, f32[96,128]{1,0:T(8,128)S(1)}, u32[]{:S(2)}, u32[]{:S(2)}) collective-permute-start(f32[96,128]{1,0:T(8,128)S(1)} %add.11), channel_id=1, source_target_pairs={{0,4},{1,5},{2,6},{3,7},{4,0},{5,1},{6,2},{7,3},{8,12},{9,13},{10,... | collective-permute-start | bytes 147464 | tf_op jit(solution)/shard_map/ppermute | solution.py:135
  88.7 5.5 %collective-permute-done.2 = f32[96,128]{1,0:T(8,128)S(1)} collective-permute-done((f32[96,128]{1,0:T(8,128)S(1)}, f32[96,128]{1,0:T(8,128)S(1)}, u32[]{:S(2)}, u32[]{:S(2)}) %collective-permute-start.2) | collective-permute-done | bytes 49184 | tf_op jit(solution)/shard_map/ppermute | solution.py:135
  94.3 11.9 %collective-permute-start.3 = (f32[96,128]{1,0:T(8,128)S(1)}, f32[96,128]{1,0:T(8,128)S(1)}, u32[]{:S(2)}, u32[]{:S(2)}) collective-permute-start(f32[96,128]{1,0:T(8,128)S(1)} %add.12), channel_id=1, source_target_pairs={{0,8},{1,9},{2,10},{3,11},{4,12},{5,13},{6,14},{7,15},{8,0},{9,1},... | collective-permute-start | bytes 147464 | tf_op jit(solution)/shard_map/ppermute | solution.py:135
  106.2 2.7 %collective-permute-done.3 = f32[96,128]{1,0:T(8,128)S(1)} collective-permute-done((f32[96,128]{1,0:T(8,128)S(1)}, f32[96,128]{1,0:T(8,128)S(1)}, u32[]{:S(2)}, u32[]{:S(2)}) %collective-permute-start.3) | collective-permute-done | bytes 49184 | tf_op jit(solution)/shard_map/ppermute | solution.py:135
  109.0 1.9 %collective-permute-start.4 = (f32[96,128]{1,0:T(8,128)S(1)}, f32[96,128]{1,0:T(8,128)S(1)}, u32[]{:S(2)}, u32[]{:S(2)}) collective-permute-start(f32[96,128]{1,0:T(8,128)S(1)} %add.13.shrink_ref), channel_id=1, source_target_pairs={{0,1},{1,0},{2,3},{3,2},{4,5},{5,4},{6,7},{7,6},{8,9},{9,8},{10,11... | collective-permute-start | bytes 147464 | tf_op jit(solution)/shard_map/ppermute | solution.py:135
  110.9 0.0 all-to-all-done.2.panels_ref
  110.9 0.0 reduce-scatter.2.cloned.1.call-done
  110.9 0.0 copy-start.2
  110.9 0.9 copy-done.2
  111.8 1.8 %shard_map.79.sum_ref = f32[192,256]{1,0:T(8,128)S(1)} custom-call(s32[1]{0:T(128)} %bitcast.me_ref, s32[192,128]{1,0:T(8,128)S(1)} %get-tuple-element.13.hold_ref, f32[96,128]{1,0:T(8,128)S(1)} %add.13.shrink_ref, bf16[32,128,256]{2,1,0:T(8,128)(2,1)S(1)} %all-to-all-done.2.panels_ref, f32[192,256]{1,0:T(8,128)S(1)} %bitcast.4), custom_call_target="tpu_custom_call" | custom-call | flops 100000000 | bytes 3145728 | tf_op jit(solution)/shard_map/pallas_call | solution.py:18
  113.7 1.2 collective-permute-done.4.shrink_ref
  114.9 2.5 %shard_map.80 = bf16[192,256]{1,0:T(8,128)(2,1)} custom-call(s32[1]{0:T(128)} %bitcast.me_ref, s32[192,128]{1,0:T(8,128)S(1)} %get-tuple-element.13.hold_ref, f32[96,128]{1,0:T(8,128)S(1)} %collective-permute-done.4.shrink_ref, bf16[32,128,256]{2,1,0:T(8,128)(2,1)S(1)} %all-to-all-done.2.panels_ref, f32[192,256]{1,0:T(8,128)S(1)} %shard_map.79.sum_ref), custom_call_target="tpu_custom_call" | custom-call | flops 22749999104 | bytes 3145728 | tf_op jit(solution)/shard_map/pallas_call | solution.py:18
  (4 shorter events, 0.0 us)
Async XLA Ops:
  7.9 14.9 %all-to-all-start = ((s32[32,1,128]{2,1,0:T(1,128)}), s32[32,1,128]{2,1,0:T(1,128)S(1)}, u32[]{:S(2)}, u32[]{:S(2)}) async-start(s32[32,1,128]{2,1,0:T(1,128)} %shard_map.73), calls=%async_computation | async-start | bytes 32768 | tf_op jit(solution)/shard_map/all_to_all | solution.py:153
  17.2 93.7 %reduce-scatter.2.cloned.1.call-start = ((), (), s32[]{:S(2)}) async-start(), calls=%async_computation.4 | async-start | bytes 3342336 | tf_op jit(solution)/shard_map/reduce_scatter | solution.py:163
  22.8 0.6 copy-start.3
  26.0 6.7 %copy-start.1 = (bf16[4,128,256]{2,1,0:T(8,128)(2,1)S(1)}, bf16[4,128,256]{2,1,0:T(8,128)(2,1)}, u32[]{:S(2)}) copy-start(bf16[4,128,256]{2,1,0:T(8,128)(2,1)} %refs_4_.1) | copy-start | bytes 786436
  26.0 6.7 %copy-start.4 = (s32[32,1,128]{2,1,0:T(1,128)S(1)}, s32[32,1,128]{2,1,0:T(1,128)}, u32[]{:S(2)}) copy-start(s32[32,1,128]{2,1,0:T(1,128)} %copy-done.3) | copy-start | bytes 49156
  26.0 6.7 %copy-start.6 = (s32[1,16]{1,0:T(1,128)S(1)}, s32[1,16]{1,0:T(1,128)}, u32[]{:S(2)}) copy-start(s32[1,16]{1,0:T(1,128)} %refs_1_.3) | copy-start | bytes 196
  26.0 6.7 %copy-start.7 = (s32[128]{0:T(128)S(1)}, s32[128]{0:T(128)}, u32[]{:S(2)}) copy-start(s32[128]{0:T(128)} %refs_2_.1) | copy-start | bytes 1540
  26.0 6.7 %copy-start.8 = (s32[64]{0:T(128)S(1)}, s32[64]{0:T(128)}, u32[]{:S(2)}) copy-start(s32[64]{0:T(128)} %refs_3_.1) | copy-start | bytes 772
  26.0 32.2 %copy-start.5 = (bf16[3,64,256]{2,1,0:T(8,128)(2,1)S(1)}, bf16[3,64,256]{2,1,0:T(8,128)(2,1)}, u32[]{:S(2)}) copy-start(bf16[3,64,256]{2,1,0:T(8,128)(2,1)} %param.7) | copy-start | bytes 294916
  26.1 32.2 %all-to-all-start.1 = ((bf16[32,256,128]{2,1,0:T(8,128)(2,1)}), bf16[32,256,128]{2,1,0:T(8,128)(2,1)S(1)}, u32[]{:S(2)}, u32[]{:S(2)}) async-start(bf16[32,256,128]{2,1,0:T(8,128)(2,1)} %shard_map.76), calls=%async_computation.1 | async-start | bytes 4194304 | tf_op jit(solution)/shard_map/all_to_all | solution.py:170
  37.3 1.3 %copy-start = (bf16[32,128,256]{2,1,0:T(8,128)(2,1)}, bf16[32,128,256]{2,1,0:T(8,128)(2,1)S(1)}, u32[]{:S(2)}) copy-start(bf16[32,128,256]{2,1,0:T(8,128)(2,1)S(1)} %get-tuple-element.18) | copy-start | bytes 6291460
  60.4 10.3 %collective-permute-start = (f32[96,128]{1,0:T(8,128)S(1)}, f32[96,128]{1,0:T(8,128)S(1)}, u32[]{:S(2)}, u32[]{:S(2)}) collective-permute-start(f32[96,128]{1,0:T(8,128)S(1)} %get-tuple-element.17), channel_id=1, source_target_pairs={{0,1},{1,0},{2,3},{3,2},{4,5},{5,4},{6,7},{7,6},{8,9},{9,8},{10,11... | collective-permute-start | bytes 147464 | tf_op jit(solution)/shard_map/ppermute | solution.py:135
  62.3 48.6 %all-to-all-start.2 = ((bf16[32,128,256]{2,1,0:T(8,128)(2,1)}), bf16[32,128,256]{2,1,0:T(8,128)(2,1)S(1)}, u32[]{:S(2)}, u32[]{:S(2)}) async-start(bf16[32,128,256]{2,1,0:T(8,128)(2,1)} %copy-done), calls=%async_computation.2 | async-start | bytes 4194304 | tf_op jit(solution)/shard_map/all_to_all | solution.py:184
  70.7 9.5 %collective-permute-start.1 = (f32[96,128]{1,0:T(8,128)S(1)}, f32[96,128]{1,0:T(8,128)S(1)}, u32[]{:S(2)}, u32[]{:S(2)}) collective-permute-start(f32[96,128]{1,0:T(8,128)S(1)} %shard_map.78), channel_id=1, source_target_pairs={{0,2},{1,3},{2,0},{3,1},{4,6},{5,7},{6,4},{7,5},{8,10},{9,11},{10,... | collective-permute-start | bytes 147464 | tf_op jit(solution)/shard_map/ppermute | solution.py:135
  80.2 14.0 %collective-permute-start.2 = (f32[96,128]{1,0:T(8,128)S(1)}, f32[96,128]{1,0:T(8,128)S(1)}, u32[]{:S(2)}, u32[]{:S(2)}) collective-permute-start(f32[96,128]{1,0:T(8,128)S(1)} %add.11), channel_id=1, source_target_pairs={{0,4},{1,5},{2,6},{3,7},{4,0},{5,1},{6,2},{7,3},{8,12},{9,13},{10,... | collective-permute-start | bytes 147464 | tf_op jit(solution)/shard_map/ppermute | solution.py:135
  94.3 14.7 %collective-permute-start.3 = (f32[96,128]{1,0:T(8,128)S(1)}, f32[96,128]{1,0:T(8,128)S(1)}, u32[]{:S(2)}, u32[]{:S(2)}) collective-permute-start(f32[96,128]{1,0:T(8,128)S(1)} %add.12), channel_id=1, source_target_pairs={{0,8},{1,9},{2,10},{3,11},{4,12},{5,13},{6,14},{7,15},{8,0},{9,1},... | collective-permute-start | bytes 147464 | tf_op jit(solution)/shard_map/ppermute | solution.py:135
  109.0 6.0 %collective-permute-start.4 = (f32[96,128]{1,0:T(8,128)S(1)}, f32[96,128]{1,0:T(8,128)S(1)}, u32[]{:S(2)}, u32[]{:S(2)}) collective-permute-start(f32[96,128]{1,0:T(8,128)S(1)} %add.13.shrink_ref), channel_id=1, source_target_pairs={{0,1},{1,0},{2,3},{3,2},{4,5},{5,4},{6,7},{7,6},{8,9},{9,8},{10,11... | collective-permute-start | bytes 147464 | tf_op jit(solution)/shard_map/ppermute | solution.py:135
  110.9 0.9 copy-start.2
Sparse Core Ops, SparseCore 0:
  21.9 81.8 reduce-scatter.1

commit v6 on v5

--- a/solution.py
+++ b/solution.py
@@ -10,7 +10,8 @@
 DMA = pltpu.SemaphoreType.DMA
 HALF_LONG = 10 ** 8
 ADD_LONG = 2*10**10
-LONG = 2275 * 10**7
+LONG = 2040 * 10**7
+PICK = 48
 ALL = 60
 
 
@@ -135,6 +136,10 @@
     return lax.ppermute(value, "tensor", [(i, i ^ bit) for i in range(size)])
 
 
+def shift(value, by, size):
+    return lax.ppermute(value, "tensor", [(i, (i + by) % size) for i in range(size)])
+
+
 def on_device(attn_out, base_weight, store_a, store_b, adapter_lists, placement_map, request_slot):
     replicas = lax.axis_size("dp")
     columns = lax.axis_size("tensor")
@@ -165,7 +170,7 @@
     asked, _ = lax.optimization_barrier((asked, partial))
     picked_a = local_call(
         pick_kernel, shaped((replicas,) + store_a.shape[1:], bf16), 0, 4 << 20,
-        [SMEM, VMEM], HBM, [DMA((replicas,))], (asked, store_a), limit=ALL,
+        [SMEM, VMEM], HBM, [DMA((replicas,))], (asked, store_a), limit=PICK,
     )
     got_a = lax.all_to_all(picked_a, "dp", split_axis=0, concat_axis=0, tiled=True)
     picked_b, hold = local_call(
@@ -180,13 +185,14 @@
         shrink_kernel, (half, half), LONG, 3 << 20,
         [SMEM] + [VMEM] * 3, (VMEM, VMEM), [pltpu.VMEM((rows, rank), f32)], (me, hold, x, got_a),
     )
-    picked_b, other = lax.optimization_barrier((picked_b, other))
+    mine = mine + across(other, 1, columns)
+    picked_b, mine = lax.optimization_barrier((picked_b, mine))
     got_b = lax.all_to_all(picked_b, "dp", split_axis=0, concat_axis=0, tiled=True)
     mine = local_call(add_kernel, half, ADD_LONG, 1 << 17, [VMEM, VMEM], VMEM, [],
-                      (mine, across(other, 1, columns)))
-    mine = mine + across(mine, 2, columns)
-    mine = mine + across(mine, 4, columns)
-    mine = mine + across(mine, 8, columns)
+                      (mine, across(mine, 2, columns)))
+    quarter = columns // 4
+    pair = mine + shift(mine, quarter, columns)
+    mine = (mine + shift(mine, -quarter, columns)) + shift(pair, quarter, columns)
     other = across(mine, 1, columns)
     def ends(kernel, cost, dtype, shrink, so_far):
         return local_call(

time: 125 us -> 122 us (0.976)
  waiting for transfers between devices: 34.5 us -> 29.4 us
  starting transfers between devices: 53.8 us -> 56.5 us
    ppermute x0 -> x3, starting transfers between devices: none -> 21.3 us  [shift(): lax.ppermute(value, 'tensor', [(i, (i + by) % size) for i in range(size)])]
    ppermute x5 -> x3, starting transfers between devices: 29.5 us -> 10.1 us  [across(): return lax.ppermute(value, 'tensor', [(i, i ^ bit) for i in range(size)])]
    ppermute x5 -> x3, waiting for transfers between devices: 13.9 us -> 4.04 us  [across(): return lax.ppermute(value, 'tensor', [(i, i ^ bit) for i in range(size)])]
    ppermute x0 -> x3, waiting for transfers between devices: none -> 4.66 us  [shift(): lax.ppermute(value, 'tensor', [(i, (i + by) % size) for i in range(size)])]
    unnamed x18 -> x16, local copies, waits for them, and re-layouts: 2.9 us -> 2.29 us
  transfers between devices with their start and end apart: 9 -> 10, of which waited for: 6 -> 6; matrix products, arithmetic and copies ran while one was open for 0% -> 0% of each run, Pallas kernels for 12% -> 13%
where the time goes in v6:
time: 122 us; the launch traced here: 121 us
  starting transfers between devices  56.5 us (46%)
  waiting for transfers between devices  29.4 us (24%)
  Pallas kernels  19.2 us (16%)
  between operations  13.6 us (11%)
  local copies, waits for them, and re-layouts  2.29 us (2%)
    ppermute x3, starting transfers between devices, shift(): lax.ppermute(value, 'tensor', [(i, (i + by) % size) for i in range(size)])  21.3 us
    all_to_all x1, waiting for transfers between devices, on_device(): lax.all_to_all(picked_a, 'dp', split_axis=0, concat_axis=0, tiled=True)  19.6 us
    pallas_call x8, Pallas kernels, local_call(): pl.pallas_call(body, out_shape=outs, grid=grid, in_specs=in_specs, out_sp...  19.2 us
    ppermute x3, starting transfers between devices, across(): return lax.ppermute(value, 'tensor', [(i, i ^ bit) for i in range(size)])  10.1 us
    all_to_all x1, starting transfers between devices, on_device(): asked = lax.all_to_all(wish, 'dp', split_axis=0, concat_axis=0, tiled=True)  9.37 us
    all_to_all x1, starting transfers between devices, on_device(): lax.all_to_all(picked_b, 'dp', split_axis=0, concat_axis=0, tiled=True)  8.15 us
    all_to_all x1, starting transfers between devices, on_device(): lax.all_to_all(picked_a, 'dp', split_axis=0, concat_axis=0, tiled=True)  7.54 us
    ppermute x3, waiting for transfers between devices, shift(): lax.ppermute(value, 'tensor', [(i, (i + by) % size) for i in range(size)])  4.66 us
  transfers between devices with their start and end apart: 10, of which 6 were waited for; matrix products, arithmetic and copies ran while one was open for 0% of the time, Pallas kernels for 13%

profile of v6, /device:TPU:6, one launch (start us, length us, event | category | flops | bytes accessed | tf_op | source)
XLA Modules:
  0.0 121.0 jit_solution(8466659053299099011)
XLA Ops:
  6.5 1.3 %shard_map.73 = s32[32,1,128]{2,1,0:T(1,128)} custom-call(s32[1,16]{1,0:T(1,128)} %refs_1_.3, s32[128]{0:T(128)} %refs_2_.1), custom_call_target="tpu_custom_call" | custom-call | bytes 16384 | tf_op jit(solution)/shard_map/pallas_call | solution.py:19
  7.9 9.4 %all-to-all-start = ((s32[32,1,128]{2,1,0:T(1,128)}), s32[32,1,128]{2,1,0:T(1,128)S(1)}, u32[]{:S(2)}, u32[]{:S(2)}) async-start(s32[32,1,128]{2,1,0:T(1,128)} %shard_map.73), calls=%async_computation | async-start | bytes 32768 | tf_op jit(solution)/shard_map/all_to_all | solution.py:158
  17.2 0.0 reduce-scatter.2.cloned.1.call-start
  17.3 4.5 %shard_map.74 = f32[16,192,256]{2,1,0:T(8,128)} custom-call(bf16[192,256]{1,0:T(8,128)(2,1)} %bitcast.5, bf16[256,4096]{1,0:T(8,128)(2,1)} %weight_ref.1), custom_call_target="tpu_custom_call" | custom-call | flops 402653184 | bytes 5242880 | tf_op jit(solution)/shard_map/pallas_call | solution.py:19
  21.8 0.0 copy-start.1
  21.8 0.0 reduce-scatter.2.cloned.1.call-update
  21.8 1.0 all-to-all-done.refs_0_.asked_ref
  22.8 0.0 copy-done.1
  22.8 2.4 %shard_map.76 = bf16[32,256,128]{2,1,0:T(8,128)(2,1)} custom-call(s32[32,1,128]{2,1,0:T(1,128)S(1)} %all-to-all-done.refs_0_.asked_ref, bf16[4,256,128]{2,1,0:T(8,128)(2,1)S(1)} %copy-done.1), custom_call_target="tpu_custom_call" | custom-call | bytes 4194304 | tf_op jit(solution)/shard_map/pallas_call | solution.py:19
  25.2 0.0 copy-start.2
  25.2 0.0 copy-start.5
  25.2 0.0 copy-start.6
  25.3 0.0 copy-start.7
  25.3 0.0 copy-start.4
  25.3 7.5 %all-to-all-start.1 = ((bf16[32,256,128]{2,1,0:T(8,128)(2,1)}), bf16[32,256,128]{2,1,0:T(8,128)(2,1)S(1)}, u32[]{:S(2)}, u32[]{:S(2)}) async-start(bf16[32,256,128]{2,1,0:T(8,128)(2,1)} %shard_map.76), calls=%async_computation.1 | async-start | bytes 4194304 | tf_op jit(solution)/shard_map/all_to_all | solution.py:175
  32.8 0.0 copy-done.2
  32.8 0.0 copy-done.5
  32.9 0.0 copy-done.6
  32.9 0.0 copy-done.7
  32.9 4.5 %shard_map.75 = (bf16[32,128,256]{2,1,0:T(8,128)(2,1)S(1)}, s32[192,128]{1,0:T(8,128)S(1)}) custom-call(s32[32,1,128]{2,1,0:T(1,128)S(1)} %all-to-all-done.refs_0_.asked_ref, s32[1,16]{1,0:T(1,128)S(1)} %copy-done.5, s32[128]{0:T(128)S(1)} %copy-done.6, s32[64]{0:T(128)S(1)} %copy-done.7, bf16[4,128,256]{2,1,0:T(8,128)(2,1)S(1)} %copy-done.2), custom_call_target="tpu_custom_call" | custom-call | bytes 4194304 | tf_op jit(solution)/shard_map/pallas_call | solution.py:19
  37.4 0.0 copy-start
  37.4 1.3 %copy-done = bf16[32,128,256]{2,1,0:T(8,128)(2,1)} copy-done((bf16[32,128,256]{2,1,0:T(8,128)(2,1)}, bf16[32,128,256]{2,1,0:T(8,128)(2,1)S(1)}, u32[]{:S(2)}) %copy-start) | copy-done | bytes 2097176
  38.8 19.6 %all-to-all-done.1.panels_ref = bf16[32,256,128]{2,1,0:T(8,128)(2,1)S(1)} async-done(((bf16[32,256,128]{2,1,0:T(8,128)(2,1)}), bf16[32,256,128]{2,1,0:T(8,128)(2,1)S(1)}, u32[]{:S(2)}, u32[]{:S(2)}) %all-to-all-start.1) | async-done | bytes 2097184 | tf_op jit(solution)/shard_map/all_to_all | solution.py:175
  58.4 0.0 copy-done.4
  58.4 2.1 %shard_map.77 = (f32[96,128]{1,0:T(8,128)S(1)}, f32[96,128]{1,0:T(8,128)S(1)}) custom-call(s32[1]{0:T(128)} %bitcast.me_ref, s32[192,128]{1,0:T(8,128)S(1)} %get-tuple-element.13.hold_ref, bf16[192,256]{1,0:T(8,128)(2,1)S(1)} %bitcast.6, bf16[32,256,128]{2,1,0:T(8,128)(2,1)S(1)} %all-to-all-done.1.panels_ref), custom_call_target="tpu_custom_call" | custom-call | flops 20400001024 | bytes 3145728 | tf_op jit(solution)/shard_map/pallas_call | solution.py:19
  60.5 1.9 %collective-permute-start = (f32[96,128]{1,0:T(8,128)S(1)}, f32[96,128]{1,0:T(8,128)S(1)}, u32[]{:S(2)}, u32[]{:S(2)}) collective-permute-start(f32[96,128]{1,0:T(8,128)S(1)} %get-tuple-element.16), channel_id=1, source_target_pairs={{0,1},{1,0},{2,3},{3,2},{4,5},{5,4},{6,7},{7,6},{8,9},{9,8},{10,11... | collective-permute-start | bytes 147464 | tf_op jit(solution)/shard_map/ppermute | solution.py:136
  62.4 4.0 %collective-permute-done = f32[96,128]{1,0:T(8,128)S(1)} collective-permute-done((f32[96,128]{1,0:T(8,128)S(1)}, f32[96,128]{1,0:T(8,128)S(1)}, u32[]{:S(2)}, u32[]{:S(2)}) %collective-permute-start) | collective-permute-done | bytes 49184 | tf_op jit(solution)/shard_map/ppermute | solution.py:136
  66.5 3.9 %collective-permute-start.1 = (f32[96,128]{1,0:T(8,128)S(1)}, f32[96,128]{1,0:T(8,128)S(1)}, u32[]{:S(2)}, u32[]{:S(2)}) collective-permute-start(f32[96,128]{1,0:T(8,128)S(1)} %add.14.a_ref), channel_id=1, source_target_pairs={{0,2},{1,3},{2,0},{3,1},{4,6},{5,7},{6,4},{7,5},{8,10},{9,11},{10,... | collective-permute-start | bytes 147464 | tf_op jit(solution)/shard_map/ppermute | solution.py:136
  70.3 8.1 %all-to-all-start.2 = ((bf16[32,128,256]{2,1,0:T(8,128)(2,1)}), bf16[32,128,256]{2,1,0:T(8,128)(2,1)S(1)}, u32[]{:S(2)}, u32[]{:S(2)}) async-start(bf16[32,128,256]{2,1,0:T(8,128)(2,1)} %copy-done), calls=%async_computation.2 | async-start | bytes 4194304 | tf_op jit(solution)/shard_map/all_to_all | solution.py:190
  78.5 0.0 collective-permute-done.1.b_ref
  78.5 9.2 %collective-permute-start.3 = (f32[96,128]{1,0:T(8,128)S(1)}, f32[96,128]{1,0:T(8,128)S(1)}, u32[]{:S(2)}, u32[]{:S(2)}) collective-permute-start(f32[96,128]{1,0:T(8,128)S(1)} %shard_map.78), channel_id=1, source_target_pairs={{0,4},{1,5},{2,6},{3,7},{4,8},{5,9},{6,10},{7,11},{8,12},{9,13},{1... | collective-permute-start | bytes 147464 | tf_op jit(solution)/shard_map/ppermute | solution.py:140
  87.7 4.3 %collective-permute-start.2 = (f32[96,128]{1,0:T(8,128)S(1)}, f32[96,128]{1,0:T(8,128)S(1)}, u32[]{:S(2)}, u32[]{:S(2)}) collective-permute-start(f32[96,128]{1,0:T(8,128)S(1)} %shard_map.78), channel_id=1, source_target_pairs={{0,12},{1,13},{2,14},{3,15},{4,0},{5,1},{6,2},{7,3},{8,4},{9,5},{1... | collective-permute-start | bytes 147464 | tf_op jit(solution)/shard_map/ppermute | solution.py:140
  92.0 1.2 collective-permute-done.3
  93.2 7.8 %collective-permute-start.4 = (f32[96,128]{1,0:T(8,128)S(1)}, f32[96,128]{1,0:T(8,128)S(1)}, u32[]{:S(2)}, u32[]{:S(2)}) collective-permute-start(f32[96,128]{1,0:T(8,128)S(1)} %add.16), channel_id=1, source_target_pairs={{0,4},{1,5},{2,6},{3,7},{4,8},{5,9},{6,10},{7,11},{8,12},{9,13},{1... | collective-permute-start | bytes 147464 | tf_op jit(solution)/shard_map/ppermute | solution.py:140
  101.0 0.1 collective-permute-done.2
  101.1 3.4 %collective-permute-done.4 = f32[96,128]{1,0:T(8,128)S(1)} collective-permute-done((f32[96,128]{1,0:T(8,128)S(1)}, f32[96,128]{1,0:T(8,128)S(1)}, u32[]{:S(2)}, u32[]{:S(2)}) %collective-permute-start.4) | collective-permute-done | bytes 49184 | tf_op jit(solution)/shard_map/ppermute | solution.py:140
  104.5 4.3 %collective-permute-start.5 = (f32[96,128]{1,0:T(8,128)S(1)}, f32[96,128]{1,0:T(8,128)S(1)}, u32[]{:S(2)}, u32[]{:S(2)}) collective-permute-start(f32[96,128]{1,0:T(8,128)S(1)} %add_add_fusion.shrink_ref), channel_id=1, source_target_pairs={{0,1},{1,0},{2,3},{3,2},{4,5},{5,4},{6,7},{7,6},{8,9},{9,8},{10,11... | collective-permute-start | bytes 147464 | tf_op jit(solution)/shard_map/ppermute | solution.py:136
  108.8 0.0 all-to-all-done.2.panels_ref
  108.8 0.0 reduce-scatter.2.cloned.1.call-done
  108.9 0.0 copy-start.3
  108.9 0.9 copy-done.3
  109.8 1.8 %shard_map.79.sum_ref = f32[192,256]{1,0:T(8,128)S(1)} custom-call(s32[1]{0:T(128)} %bitcast.me_ref, s32[192,128]{1,0:T(8,128)S(1)} %get-tuple-element.13.hold_ref, f32[96,128]{1,0:T(8,128)S(1)} %add_add_fusion.shrink_ref, bf16[32,128,256]{2,1,0:T(8,128)(2,1)S(1)} %all-to-all-done.2.panels_ref, f32[192,256]{1,0:T(8,128)S(1)} %bitcast.4), custom_call_target="tpu_custom_call" | custom-call | flops 100000000 | bytes 3145728 | tf_op jit(solution)/shard_map/pallas_call | solution.py:19
  111.6 0.0 collective-permute-done.5.shrink_ref
  111.6 2.5 %shard_map.80 = bf16[192,256]{1,0:T(8,128)(2,1)} custom-call(s32[1]{0:T(128)} %bitcast.me_ref, s32[192,128]{1,0:T(8,128)S(1)} %get-tuple-element.13.hold_ref, f32[96,128]{1,0:T(8,128)S(1)} %collective-permute-done.5.shrink_ref, bf16[32,128,256]{2,1,0:T(8,128)(2,1)S(1)} %all-to-all-done.2.panels_ref, f32[192,256]{1,0:T(8,128)S(1)} %shard_map.79.sum_ref), custom_call_target="tpu_custom_call" | custom-call | flops 20400001024 | bytes 3145728 | tf_op jit(solution)/shard_map/pallas_call | solution.py:19
  (4 shorter events, 0.0 us)
Async XLA Ops:
  7.9 14.9 %all-to-all-start = ((s32[32,1,128]{2,1,0:T(1,128)}), s32[32,1,128]{2,1,0:T(1,128)S(1)}, u32[]{:S(2)}, u32[]{:S(2)}) async-start(s32[32,1,128]{2,1,0:T(1,128)} %shard_map.73), calls=%async_computation | async-start | bytes 32768 | tf_op jit(solution)/shard_map/all_to_all | solution.py:158
  17.2 91.6 %reduce-scatter.2.cloned.1.call-start = ((), (), s32[]{:S(2)}) async-start(), calls=%async_computation.4 | async-start | bytes 3342336 | tf_op jit(solution)/shard_map/reduce_scatter | solution.py:168
  21.8 1.0 copy-start.1
  25.2 7.6 %copy-start.2 = (bf16[4,128,256]{2,1,0:T(8,128)(2,1)S(1)}, bf16[4,128,256]{2,1,0:T(8,128)(2,1)}, u32[]{:S(2)}) copy-start(bf16[4,128,256]{2,1,0:T(8,128)(2,1)} %refs_4_.1) | copy-start | bytes 786436
  25.2 7.6 %copy-start.5 = (s32[1,16]{1,0:T(1,128)S(1)}, s32[1,16]{1,0:T(1,128)}, u32[]{:S(2)}) copy-start(s32[1,16]{1,0:T(1,128)} %refs_1_.3) | copy-start | bytes 196
  25.2 7.6 %copy-start.6 = (s32[128]{0:T(128)S(1)}, s32[128]{0:T(128)}, u32[]{:S(2)}) copy-start(s32[128]{0:T(128)} %refs_2_.1) | copy-start | bytes 1540
  25.3 7.6 %copy-start.7 = (s32[64]{0:T(128)S(1)}, s32[64]{0:T(128)}, u32[]{:S(2)}) copy-start(s32[64]{0:T(128)} %refs_3_.1) | copy-start | bytes 772
  25.3 33.1 %copy-start.4 = (bf16[3,64,256]{2,1,0:T(8,128)(2,1)S(1)}, bf16[3,64,256]{2,1,0:T(8,128)(2,1)}, u32[]{:S(2)}) copy-start(bf16[3,64,256]{2,1,0:T(8,128)(2,1)} %param.7) | copy-start | bytes 294916
  25.3 33.1 %all-to-all-start.1 = ((bf16[32,256,128]{2,1,0:T(8,128)(2,1)}), bf16[32,256,128]{2,1,0:T(8,128)(2,1)S(1)}, u32[]{:S(2)}, u32[]{:S(2)}) async-start(bf16[32,256,128]{2,1,0:T(8,128)(2,1)} %shard_map.76), calls=%async_computation.1 | async-start | bytes 4194304 | tf_op jit(solution)/shard_map/all_to_all | solution.py:175
  37.4 1.3 %copy-start = (bf16[32,128,256]{2,1,0:T(8,128)(2,1)}, bf16[32,128,256]{2,1,0:T(8,128)(2,1)S(1)}, u32[]{:S(2)}) copy-start(bf16[32,128,256]{2,1,0:T(8,128)(2,1)S(1)} %get-tuple-element.18) | copy-start | bytes 6291460
  60.5 6.0 %collective-permute-start = (f32[96,128]{1,0:T(8,128)S(1)}, f32[96,128]{1,0:T(8,128)S(1)}, u32[]{:S(2)}, u32[]{:S(2)}) collective-permute-start(f32[96,128]{1,0:T(8,128)S(1)} %get-tuple-element.16), channel_id=1, source_target_pairs={{0,1},{1,0},{2,3},{3,2},{4,5},{5,4},{6,7},{7,6},{8,9},{9,8},{10,11... | collective-permute-start | bytes 147464 | tf_op jit(solution)/shard_map/ppermute | solution.py:136
  66.5 12.0 %collective-permute-start.1 = (f32[96,128]{1,0:T(8,128)S(1)}, f32[96,128]{1,0:T(8,128)S(1)}, u32[]{:S(2)}, u32[]{:S(2)}) collective-permute-start(f32[96,128]{1,0:T(8,128)S(1)} %add.14.a_ref), channel_id=1, source_target_pairs={{0,2},{1,3},{2,0},{3,1},{4,6},{5,7},{6,4},{7,5},{8,10},{9,11},{10,... | collective-permute-start | bytes 147464 | tf_op jit(solution)/shard_map/ppermute | solution.py:136
  70.3 38.5 %all-to-all-start.2 = ((bf16[32,128,256]{2,1,0:T(8,128)(2,1)}), bf16[32,128,256]{2,1,0:T(8,128)(2,1)S(1)}, u32[]{:S(2)}, u32[]{:S(2)}) async-start(bf16[32,128,256]{2,1,0:T(8,128)(2,1)} %copy-done), calls=%async_computation.2 | async-start | bytes 4194304 | tf_op jit(solution)/shard_map/all_to_all | solution.py:190
  78.5 14.6 %collective-permute-start.3 = (f32[96,128]{1,0:T(8,128)S(1)}, f32[96,128]{1,0:T(8,128)S(1)}, u32[]{:S(2)}, u32[]{:S(2)}) collective-permute-start(f32[96,128]{1,0:T(8,128)S(1)} %shard_map.78), channel_id=1, source_target_pairs={{0,4},{1,5},{2,6},{3,7},{4,8},{5,9},{6,10},{7,11},{8,12},{9,13},{1... | collective-permute-start | bytes 147464 | tf_op jit(solution)/shard_map/ppermute | solution.py:140
  87.7 13.3 %collective-permute-start.2 = (f32[96,128]{1,0:T(8,128)S(1)}, f32[96,128]{1,0:T(8,128)S(1)}, u32[]{:S(2)}, u32[]{:S(2)}) collective-permute-start(f32[96,128]{1,0:T(8,128)S(1)} %shard_map.78), channel_id=1, source_target_pairs={{0,12},{1,13},{2,14},{3,15},{4,0},{5,1},{6,2},{7,3},{8,4},{9,5},{1... | collective-permute-start | bytes 147464 | tf_op jit(solution)/shard_map/ppermute | solution.py:140
  93.2 11.3 %collective-permute-start.4 = (f32[96,128]{1,0:T(8,128)S(1)}, f32[96,128]{1,0:T(8,128)S(1)}, u32[]{:S(2)}, u32[]{:S(2)}) collective-permute-start(f32[96,128]{1,0:T(8,128)S(1)} %add.16), channel_id=1, source_target_pairs={{0,4},{1,5},{2,6},{3,7},{4,8},{5,9},{6,10},{7,11},{8,12},{9,13},{1... | collective-permute-start | bytes 147464 | tf_op jit(solution)/shard_map/ppermute | solution.py:140
  104.5 7.1 %collective-permute-start.5 = (f32[96,128]{1,0:T(8,128)S(1)}, f32[96,128]{1,0:T(8,128)S(1)}, u32[]{:S(2)}, u32[]{:S(2)}) collective-permute-start(f32[96,128]{1,0:T(8,128)S(1)} %add_add_fusion.shrink_ref), channel_id=1, source_target_pairs={{0,1},{1,0},{2,3},{3,2},{4,5},{5,4},{6,7},{7,6},{8,9},{9,8},{10,11... | collective-permute-start | bytes 147464 | tf_op jit(solution)/shard_map/ppermute | solution.py:136
  108.9 0.9 copy-start.3
Sparse Core Ops, SparseCore 0:
  21.9 85.9 reduce-scatter.1

commit v7 on v6

--- a/solution.py
+++ b/solution.py
@@ -79,7 +79,7 @@
     x = x_ref[...]
     total_ref[...] = jnp.zeros_like(total_ref)
 
-    @pl.loop(0, panels_ref.shape[0], unroll=4)
+    @pl.loop(0, panels_ref.shape[0], unroll=16)
     def _(q):
         product = jnp.dot(x, panels_ref[q], preferred_element_type=jnp.float32)
         total_ref[...] = jnp.where(hold == q, product, total_ref[...])
@@ -109,7 +109,7 @@
     both = jnp.concatenate([high, low], axis=1)
     total_ref[...] = jnp.zeros_like(total_ref)
 
-    @pl.loop(0, panels_ref.shape[0], unroll=4)
+    @pl.loop(0, panels_ref.shape[0], unroll=16)
     def _(q):
         panel = panels_ref[q]
         product = jnp.dot(

time: 122 us -> 120 us (0.984)
  Pallas kernels: 19.2 us -> 16.5 us
    pallas_call x8, Pallas kernels: 19.2 us -> 16.5 us  [local_call(): pl.pallas_call(body, out_shape=outs, grid=grid, in_specs=in_specs, out_sp...]
  transfers between devices with their start and end apart: 10 -> 10, of which waited for: 6 -> 6; matrix products, arithmetic and copies ran while one was open for 0% -> 0% of each run, Pallas kernels for 13% -> 11%
where the time goes in v7:
time: 120 us; the launch traced here: 119 us
  starting transfers between devices  56 us (47%)
  waiting for transfers between devices  30.4 us (25%)
  Pallas kernels  16.5 us (14%)
  between operations  13.6 us (11%)
  local copies, waits for them, and re-layouts  2.29 us (2%)
    ppermute x3, starting transfers between devices, shift(): lax.ppermute(value, 'tensor', [(i, (i + by) % size) for i in range(size)])  21.2 us
    all_to_all x1, waiting for transfers between devices, on_device(): lax.all_to_all(picked_a, 'dp', split_axis=0, concat_axis=0, tiled=True)  19.6 us
    pallas_call x8, Pallas kernels, local_call(): pl.pallas_call(body, out_shape=outs, grid=grid, in_specs=in_specs, out_sp...  16.5 us
    ppermute x3, starting transfers between devices, across(): return lax.ppermute(value, 'tensor', [(i, i ^ bit) for i in range(size)])  9.53 us
    all_to_all x1, starting transfers between devices, on_device(): asked = lax.all_to_all(wish, 'dp', split_axis=0, concat_axis=0, tiled=True)  9.37 us
    all_to_all x1, starting transfers between devices, on_device(): lax.all_to_all(picked_b, 'dp', split_axis=0, concat_axis=0, tiled=True)  8.36 us
    all_to_all x1, starting transfers between devices, on_device(): lax.all_to_all(picked_a, 'dp', split_axis=0, concat_axis=0, tiled=True)  7.54 us
    ppermute x3, waiting for transfers between devices, shift(): lax.ppermute(value, 'tensor', [(i, (i + by) % size) for i in range(size)])  5.19 us
  transfers between devices with their start and end apart: 10, of which 6 were waited for; matrix products, arithmetic and copies ran while one was open for 0% of the time, Pallas kernels for 11%

profile of v7, /device:TPU:6, one launch (start us, length us, event | category | flops | bytes accessed | tf_op | source)
XLA Modules:
  0.0 118.9 jit_solution(2103693858170862884)
XLA Ops:
  6.5 1.3 %shard_map.73 = s32[32,1,128]{2,1,0:T(1,128)} custom-call(s32[1,16]{1,0:T(1,128)} %refs_1_.3, s32[128]{0:T(128)} %refs_2_.1), custom_call_target="tpu_custom_call" | custom-call | bytes 16384 | tf_op jit(solution)/shard_map/pallas_call | solution.py:19
  7.9 9.4 %all-to-all-start = ((s32[32,1,128]{2,1,0:T(1,128)}), s32[32,1,128]{2,1,0:T(1,128)S(1)}, u32[]{:S(2)}, u32[]{:S(2)}) async-start(s32[32,1,128]{2,1,0:T(1,128)} %shard_map.73), calls=%async_computation | async-start | bytes 32768 | tf_op jit(solution)/shard_map/all_to_all | solution.py:158
  17.2 0.0 reduce-scatter.2.cloned.1.call-start
  17.3 4.5 %shard_map.74 = f32[16,192,256]{2,1,0:T(8,128)} custom-call(bf16[192,256]{1,0:T(8,128)(2,1)} %bitcast.5, bf16[256,4096]{1,0:T(8,128)(2,1)} %weight_ref.1), custom_call_target="tpu_custom_call" | custom-call | flops 402653184 | bytes 5242880 | tf_op jit(solution)/shard_map/pallas_call | solution.py:19
  21.8 0.0 copy-start.1
  21.8 0.0 reduce-scatter.2.cloned.1.call-update
  21.8 1.0 all-to-all-done.refs_0_.asked_ref
  22.8 0.0 copy-done.1
  22.8 2.4 %shard_map.76 = bf16[32,256,128]{2,1,0:T(8,128)(2,1)} custom-call(s32[32,1,128]{2,1,0:T(1,128)S(1)} %all-to-all-done.refs_0_.asked_ref, bf16[4,256,128]{2,1,0:T(8,128)(2,1)S(1)} %copy-done.1), custom_call_target="tpu_custom_call" | custom-call | bytes 4194304 | tf_op jit(solution)/shard_map/pallas_call | solution.py:19
  25.2 0.0 copy-start.2
  25.2 0.0 copy-start.5
  25.2 0.0 copy-start.6
  25.3 0.0 copy-start.7
  25.3 0.0 copy-start.4
  25.3 7.5 %all-to-all-start.1 = ((bf16[32,256,128]{2,1,0:T(8,128)(2,1)}), bf16[32,256,128]{2,1,0:T(8,128)(2,1)S(1)}, u32[]{:S(2)}, u32[]{:S(2)}) async-start(bf16[32,256,128]{2,1,0:T(8,128)(2,1)} %shard_map.76), calls=%async_computation.1 | async-start | bytes 4194304 | tf_op jit(solution)/shard_map/all_to_all | solution.py:175
  32.8 0.0 copy-done.2
  32.8 0.0 copy-done.5
  32.9 0.0 copy-done.6
  32.9 0.0 copy-done.7
  32.9 4.5 %shard_map.75 = (bf16[32,128,256]{2,1,0:T(8,128)(2,1)S(1)}, s32[192,128]{1,0:T(8,128)S(1)}) custom-call(s32[32,1,128]{2,1,0:T(1,128)S(1)} %all-to-all-done.refs_0_.asked_ref, s32[1,16]{1,0:T(1,128)S(1)} %copy-done.5, s32[128]{0:T(128)S(1)} %copy-done.6, s32[64]{0:T(128)S(1)} %copy-done.7, bf16[4,128,256]{2,1,0:T(8,128)(2,1)S(1)} %copy-done.2), custom_call_target="tpu_custom_call" | custom-call | bytes 4194304 | tf_op jit(solution)/shard_map/pallas_call | solution.py:19
  37.4 0.0 copy-start
  37.4 1.3 %copy-done = bf16[32,128,256]{2,1,0:T(8,128)(2,1)} copy-done((bf16[32,128,256]{2,1,0:T(8,128)(2,1)}, bf16[32,128,256]{2,1,0:T(8,128)(2,1)S(1)}, u32[]{:S(2)}) %copy-start) | copy-done | bytes 2097176
  38.8 19.6 %all-to-all-done.1.panels_ref = bf16[32,256,128]{2,1,0:T(8,128)(2,1)S(1)} async-done(((bf16[32,256,128]{2,1,0:T(8,128)(2,1)}), bf16[32,256,128]{2,1,0:T(8,128)(2,1)S(1)}, u32[]{:S(2)}, u32[]{:S(2)}) %all-to-all-start.1) | async-done | bytes 2097184 | tf_op jit(solution)/shard_map/all_to_all | solution.py:175
  58.4 0.0 copy-done.4
  58.4 1.2 shard_map.77
  59.6 2.0 %collective-permute-start = (f32[96,128]{1,0:T(8,128)S(1)}, f32[96,128]{1,0:T(8,128)S(1)}, u32[]{:S(2)}, u32[]{:S(2)}) collective-permute-start(f32[96,128]{1,0:T(8,128)S(1)} %get-tuple-element.16), channel_id=1, source_target_pairs={{0,1},{1,0},{2,3},{3,2},{4,5},{5,4},{6,7},{7,6},{8,9},{9,8},{10,11... | collective-permute-start | bytes 147464 | tf_op jit(solution)/shard_map/ppermute | solution.py:136
  61.5 4.0 %collective-permute-done = f32[96,128]{1,0:T(8,128)S(1)} collective-permute-done((f32[96,128]{1,0:T(8,128)S(1)}, f32[96,128]{1,0:T(8,128)S(1)}, u32[]{:S(2)}, u32[]{:S(2)}) %collective-permute-start) | collective-permute-done | bytes 49184 | tf_op jit(solution)/shard_map/ppermute | solution.py:136
  65.6 4.0 %collective-permute-start.1 = (f32[96,128]{1,0:T(8,128)S(1)}, f32[96,128]{1,0:T(8,128)S(1)}, u32[]{:S(2)}, u32[]{:S(2)}) collective-permute-start(f32[96,128]{1,0:T(8,128)S(1)} %add.14.a_ref), channel_id=1, source_target_pairs={{0,2},{1,3},{2,0},{3,1},{4,6},{5,7},{6,4},{7,5},{8,10},{9,11},{10,... | collective-permute-start | bytes 147464 | tf_op jit(solution)/shard_map/ppermute | solution.py:136
  69.6 8.4 %all-to-all-start.2 = ((bf16[32,128,256]{2,1,0:T(8,128)(2,1)}), bf16[32,128,256]{2,1,0:T(8,128)(2,1)S(1)}, u32[]{:S(2)}, u32[]{:S(2)}) async-start(bf16[32,128,256]{2,1,0:T(8,128)(2,1)} %copy-done), calls=%async_computation.2 | async-start | bytes 4194304 | tf_op jit(solution)/shard_map/all_to_all | solution.py:190
  78.0 0.0 collective-permute-done.1.b_ref
  78.0 8.6 %collective-permute-start.3 = (f32[96,128]{1,0:T(8,128)S(1)}, f32[96,128]{1,0:T(8,128)S(1)}, u32[]{:S(2)}, u32[]{:S(2)}) collective-permute-start(f32[96,128]{1,0:T(8,128)S(1)} %shard_map.78), channel_id=1, source_target_pairs={{0,4},{1,5},{2,6},{3,7},{4,8},{5,9},{6,10},{7,11},{8,12},{9,13},{1... | collective-permute-start | bytes 147464 | tf_op jit(solution)/shard_map/ppermute | solution.py:140
  86.6 4.0 %collective-permute-start.2 = (f32[96,128]{1,0:T(8,128)S(1)}, f32[96,128]{1,0:T(8,128)S(1)}, u32[]{:S(2)}, u32[]{:S(2)}) collective-permute-start(f32[96,128]{1,0:T(8,128)S(1)} %shard_map.78), channel_id=1, source_target_pairs={{0,12},{1,13},{2,14},{3,15},{4,0},{5,1},{6,2},{7,3},{8,4},{9,5},{1... | collective-permute-start | bytes 147464 | tf_op jit(solution)/shard_map/ppermute | solution.py:140
  90.6 1.2 %collective-permute-done.3 = f32[96,128]{1,0:T(8,128)S(1)} collective-permute-done((f32[96,128]{1,0:T(8,128)S(1)}, f32[96,128]{1,0:T(8,128)S(1)}, u32[]{:S(2)}, u32[]{:S(2)}) %collective-permute-start.3) | collective-permute-done | bytes 49184 | tf_op jit(solution)/shard_map/ppermute | solution.py:140
  91.8 8.6 %collective-permute-start.4 = (f32[96,128]{1,0:T(8,128)S(1)}, f32[96,128]{1,0:T(8,128)S(1)}, u32[]{:S(2)}, u32[]{:S(2)}) collective-permute-start(f32[96,128]{1,0:T(8,128)S(1)} %add.16), channel_id=1, source_target_pairs={{0,4},{1,5},{2,6},{3,7},{4,8},{5,9},{6,10},{7,11},{8,12},{9,13},{1... | collective-permute-start | bytes 147464 | tf_op jit(solution)/shard_map/ppermute | solution.py:140
  100.4 0.0 collective-permute-done.2
  100.4 4.0 %collective-permute-done.4 = f32[96,128]{1,0:T(8,128)S(1)} collective-permute-done((f32[96,128]{1,0:T(8,128)S(1)}, f32[96,128]{1,0:T(8,128)S(1)}, u32[]{:S(2)}, u32[]{:S(2)}) %collective-permute-start.4) | collective-permute-done | bytes 49184 | tf_op jit(solution)/shard_map/ppermute | solution.py:140
  104.4 3.5 %collective-permute-start.5 = (f32[96,128]{1,0:T(8,128)S(1)}, f32[96,128]{1,0:T(8,128)S(1)}, u32[]{:S(2)}, u32[]{:S(2)}) collective-permute-start(f32[96,128]{1,0:T(8,128)S(1)} %add_add_fusion.shrink_ref), channel_id=1, source_target_pairs={{0,1},{1,0},{2,3},{3,2},{4,5},{5,4},{6,7},{7,6},{8,9},{9,8},{10,11... | collective-permute-start | bytes 147464 | tf_op jit(solution)/shard_map/ppermute | solution.py:136
  108.0 0.0 all-to-all-done.2.panels_ref
  108.0 0.0 reduce-scatter.2.cloned.1.call-done
  108.0 0.0 copy-start.3
  108.0 0.9 copy-done.3
  108.9 1.0 shard_map.79.sum_ref
  109.9 0.5 collective-permute-done.5.shrink_ref
  110.4 1.6 %shard_map.80 = bf16[192,256]{1,0:T(8,128)(2,1)} custom-call(s32[1]{0:T(128)} %bitcast.me_ref, s32[192,128]{1,0:T(8,128)S(1)} %get-tuple-element.13.hold_ref, f32[96,128]{1,0:T(8,128)S(1)} %collective-permute-done.5.shrink_ref, bf16[32,128,256]{2,1,0:T(8,128)(2,1)S(1)} %all-to-all-done.2.panels_ref, f32[192,256]{1,0:T(8,128)S(1)} %shard_map.79.sum_ref), custom_call_target="tpu_custom_call" | custom-call | flops 20400001024 | bytes 3145728 | tf_op jit(solution)/shard_map/pallas_call | solution.py:19
  (4 shorter events, 0.0 us)
Async XLA Ops:
  7.9 14.9 %all-to-all-start = ((s32[32,1,128]{2,1,0:T(1,128)}), s32[32,1,128]{2,1,0:T(1,128)S(1)}, u32[]{:S(2)}, u32[]{:S(2)}) async-start(s32[32,1,128]{2,1,0:T(1,128)} %shard_map.73), calls=%async_computation | async-start | bytes 32768 | tf_op jit(solution)/shard_map/all_to_all | solution.py:158
  17.2 90.8 %reduce-scatter.2.cloned.1.call-start = ((), (), s32[]{:S(2)}) async-start(), calls=%async_computation.4 | async-start | bytes 3342336 | tf_op jit(solution)/shard_map/reduce_scatter | solution.py:168
  21.8 1.0 copy-start.1
  25.2 7.6 %copy-start.2 = (bf16[4,128,256]{2,1,0:T(8,128)(2,1)S(1)}, bf16[4,128,256]{2,1,0:T(8,128)(2,1)}, u32[]{:S(2)}) copy-start(bf16[4,128,256]{2,1,0:T(8,128)(2,1)} %refs_4_.1) | copy-start | bytes 786436
  25.2 7.6 %copy-start.5 = (s32[1,16]{1,0:T(1,128)S(1)}, s32[1,16]{1,0:T(1,128)}, u32[]{:S(2)}) copy-start(s32[1,16]{1,0:T(1,128)} %refs_1_.3) | copy-start | bytes 196
  25.2 7.6 %copy-start.6 = (s32[128]{0:T(128)S(1)}, s32[128]{0:T(128)}, u32[]{:S(2)}) copy-start(s32[128]{0:T(128)} %refs_2_.1) | copy-start | bytes 1540
  25.3 7.6 %copy-start.7 = (s32[64]{0:T(128)S(1)}, s32[64]{0:T(128)}, u32[]{:S(2)}) copy-start(s32[64]{0:T(128)} %refs_3_.1) | copy-start | bytes 772
  25.3 33.1 %copy-start.4 = (bf16[3,64,256]{2,1,0:T(8,128)(2,1)S(1)}, bf16[3,64,256]{2,1,0:T(8,128)(2,1)}, u32[]{:S(2)}) copy-start(bf16[3,64,256]{2,1,0:T(8,128)(2,1)} %param.7) | copy-start | bytes 294916
  25.3 33.1 %all-to-all-start.1 = ((bf16[32,256,128]{2,1,0:T(8,128)(2,1)}), bf16[32,256,128]{2,1,0:T(8,128)(2,1)S(1)}, u32[]{:S(2)}, u32[]{:S(2)}) async-start(bf16[32,256,128]{2,1,0:T(8,128)(2,1)} %shard_map.76), calls=%async_computation.1 | async-start | bytes 4194304 | tf_op jit(solution)/shard_map/all_to_all | solution.py:175
  37.4 1.3 %copy-start = (bf16[32,128,256]{2,1,0:T(8,128)(2,1)}, bf16[32,128,256]{2,1,0:T(8,128)(2,1)S(1)}, u32[]{:S(2)}) copy-start(bf16[32,128,256]{2,1,0:T(8,128)(2,1)S(1)} %get-tuple-element.18) | copy-start | bytes 6291460
  59.6 6.0 %collective-permute-start = (f32[96,128]{1,0:T(8,128)S(1)}, f32[96,128]{1,0:T(8,128)S(1)}, u32[]{:S(2)}, u32[]{:S(2)}) collective-permute-start(f32[96,128]{1,0:T(8,128)S(1)} %get-tuple-element.16), channel_id=1, source_target_pairs={{0,1},{1,0},{2,3},{3,2},{4,5},{5,4},{6,7},{7,6},{8,9},{9,8},{10,11... | collective-permute-start | bytes 147464 | tf_op jit(solution)/shard_map/ppermute | solution.py:136
  65.6 12.4 %collective-permute-start.1 = (f32[96,128]{1,0:T(8,128)S(1)}, f32[96,128]{1,0:T(8,128)S(1)}, u32[]{:S(2)}, u32[]{:S(2)}) collective-permute-start(f32[96,128]{1,0:T(8,128)S(1)} %add.14.a_ref), channel_id=1, source_target_pairs={{0,2},{1,3},{2,0},{3,1},{4,6},{5,7},{6,4},{7,5},{8,10},{9,11},{10,... | collective-permute-start | bytes 147464 | tf_op jit(solution)/shard_map/ppermute | solution.py:136
  69.6 38.4 %all-to-all-start.2 = ((bf16[32,128,256]{2,1,0:T(8,128)(2,1)}), bf16[32,128,256]{2,1,0:T(8,128)(2,1)S(1)}, u32[]{:S(2)}, u32[]{:S(2)}) async-start(bf16[32,128,256]{2,1,0:T(8,128)(2,1)} %copy-done), calls=%async_computation.2 | async-start | bytes 4194304 | tf_op jit(solution)/shard_map/all_to_all | solution.py:190
  78.0 13.8 %collective-permute-start.3 = (f32[96,128]{1,0:T(8,128)S(1)}, f32[96,128]{1,0:T(8,128)S(1)}, u32[]{:S(2)}, u32[]{:S(2)}) collective-permute-start(f32[96,128]{1,0:T(8,128)S(1)} %shard_map.78), channel_id=1, source_target_pairs={{0,4},{1,5},{2,6},{3,7},{4,8},{5,9},{6,10},{7,11},{8,12},{9,13},{1... | collective-permute-start | bytes 147464 | tf_op jit(solution)/shard_map/ppermute | solution.py:140
  86.6 13.8 %collective-permute-start.2 = (f32[96,128]{1,0:T(8,128)S(1)}, f32[96,128]{1,0:T(8,128)S(1)}, u32[]{:S(2)}, u32[]{:S(2)}) collective-permute-start(f32[96,128]{1,0:T(8,128)S(1)} %shard_map.78), channel_id=1, source_target_pairs={{0,12},{1,13},{2,14},{3,15},{4,0},{5,1},{6,2},{7,3},{8,4},{9,5},{1... | collective-permute-start | bytes 147464 | tf_op jit(solution)/shard_map/ppermute | solution.py:140
  91.8 12.6 %collective-permute-start.4 = (f32[96,128]{1,0:T(8,128)S(1)}, f32[96,128]{1,0:T(8,128)S(1)}, u32[]{:S(2)}, u32[]{:S(2)}) collective-permute-start(f32[96,128]{1,0:T(8,128)S(1)} %add.16), channel_id=1, source_target_pairs={{0,4},{1,5},{2,6},{3,7},{4,8},{5,9},{6,10},{7,11},{8,12},{9,13},{1... | collective-permute-start | bytes 147464 | tf_op jit(solution)/shard_map/ppermute | solution.py:140
  104.4 6.0 %collective-permute-start.5 = (f32[96,128]{1,0:T(8,128)S(1)}, f32[96,128]{1,0:T(8,128)S(1)}, u32[]{:S(2)}, u32[]{:S(2)}) collective-permute-start(f32[96,128]{1,0:T(8,128)S(1)} %add_add_fusion.shrink_ref), channel_id=1, source_target_pairs={{0,1},{1,0},{2,3},{3,2},{4,5},{5,4},{6,7},{7,6},{8,9},{9,8},{10,11... | collective-permute-start | bytes 147464 | tf_op jit(solution)/shard_map/ppermute | solution.py:136
  108.0 0.9 copy-start.3
Sparse Core Ops, SparseCore 0:
  21.9 85.3 reduce-scatter.1
